TPU v7x, 32 devices: a whole 2x2x4 slice. The times are simulated.
32 devices in a mesh: dp: 16 (over z, x, core), seq: 2 (over y).
Axes of the slice: x: 2, y: 2, z: 4, core: 2. Of those that a mesh axis runs over, the one named last changes fastest.
Arguments:
- tokens: bfloat16 [16, 16, 256, 512], P('dp', None, 'seq'), may hold values from -6 to 6
- lengths: int32 [16, 2, 3], P('dp'), may hold values from 1 to 5, 8 in all within a row
- cotangent: bfloat16 [16, 16, 256, 512], P('dp', None, 'seq'), may hold values from -8 to 8
- norm_gain: bfloat16 [2, 2, 512], P(None, None, ('dp', 'seq')), may hold values from 0.25 to 1.75
- norm_bias: bfloat16 [2, 2, 512], P(None, None, ('dp', 'seq')), may hold values from -3 to 3
- w_qkv: bfloat16 [2, 512, 1536], P(None, ('dp', 'seq')), may hold values from -0.25 to 0.25
- w_proj: bfloat16 [2, 512, 512], P(None, ('dp', 'seq')), may hold values from -0.75 to 0.75
- w_in: bfloat16 [2, 512, 2048], P(None, ('dp', 'seq')), may hold values from -0.25 to 0.25
- b_in: bfloat16 [2, 2048], P(None, ('dp', 'seq')), may hold values from -3 to 3
- w_out: bfloat16 [2, 2048, 512], P(None, ('dp', 'seq')), may hold values from -0.125 to 0.125
Outputs:
- activations: bfloat16 [16, 16, 256, 512], P('dp', None, 'seq')
- grad_tokens: bfloat16 [16, 16, 256, 512], P('dp', None, 'seq')
- grad_norm_gain: float32 [2, 2, 512], P(None, None, ('dp', 'seq'))
- grad_norm_bias: float32 [2, 2, 512], P(None, None, ('dp', 'seq'))
- grad_w_qkv: float32 [2, 512, 1536], P(None, ('dp', 'seq'))
- grad_w_proj: float32 [2, 512, 512], P(None, ('dp', 'seq'))
- grad_w_in: float32 [2, 512, 2048], P(None, ('dp', 'seq'))
- grad_b_in: float32 [2, 2048], P(None, ('dp', 'seq'))
- grad_w_out: float32 [2, 2048, 512], P(None, ('dp', 'seq'))
Inputs may be any that keep to these rules, and one draw needn't show every extreme that they name: In each group, the 3 clip lengths of each of the 2 micro-batches sum to 8; in each micro-batch the longest clip has exactly 5 steps.
All inputs are finite; a program needn't handle non-finite values.
Results may differ from a plain program's by a relative error of at most 0.017.
Values may be sent and summed in bfloat16 or wider, within the bound.
No kernel may reach another device: no remote copies, remote signals or barrier semaphores. Data moves between devices by JAX's collectives and lax.ppermute only.
A program may use at most 320 MiB of HBM per device.

v0:
```python
import jax
import jax.numpy as jnp
from jax import lax
from jax.sharding import PartitionSpec as P

HEADS = 8
MICRO = 2


def norm_stats(values):
    centre = values - jnp.mean(values, -1, keepdims=True)
    variance = jnp.mean(centre * centre, -1, keepdims=True)
    inverse = lax.rsqrt(variance + 1e-05)
    return (centre * inverse, inverse)


def norm_back(grad_scaled, unit_rows, inverse):
    mean_grad = jnp.mean(grad_scaled, -1, keepdims=True)
    mean_cross = jnp.mean(grad_scaled * unit_rows, -1, keepdims=True)
    return inverse * (grad_scaled - mean_grad - unit_rows * mean_cross)


def apply_right(row_data, matrix):
    return jnp.einsum("...k,kn->...n", row_data, matrix, preferred_element_type=jnp.float32)


def apply_left(row_data, matrix):
    return jnp.einsum("...n,kn->...k", row_data, matrix, preferred_element_type=jnp.float32)


def outer_sum(left_rows, right_rows):
    flat_left = left_rows.reshape(-1, left_rows.shape[-1])
    flat_right = right_rows.reshape(-1, right_rows.shape[-1])
    return jnp.einsum("rk,rn->kn", flat_left, flat_right, preferred_element_type=jnp.float32)


def row_total(values):
    return jnp.sum(values.reshape(-1, values.shape[-1]), 0)


def gelu_smooth(values):
    return 0.5 * values * (1.0 + lax.erf(values * 0.7071067811865476))


def gelu_slope(values):
    return (
        0.5 * (1.0 + lax.erf(values * 0.7071067811865476))
        + values * jnp.exp(-0.5 * values * values) * 0.3989422804014327
    )


def clip_mask(lengths_micro, steps_n):
    clip_ends = jnp.cumsum(lengths_micro, -1)
    positions = jnp.arange(steps_n, dtype=jnp.int32)
    clip_ids = jnp.sum((positions[None, :, None] >= clip_ends[:, None, :]).astype(jnp.int32), -1)
    same_clip = clip_ids[:, :, None] == clip_ids[:, None, :]
    return same_clip & (positions[None, None, :] <= positions[None, :, None])


def spatial_forward(parts_qkv):
    queries, key_rows, values = parts_qkv
    scale_factor = queries.shape[-1] ** (-0.5)
    scores = (
        jnp.einsum("fphe,fqhe->fhpq", queries, key_rows, preferred_element_type=jnp.float32)
        * scale_factor
    )
    row_top = jnp.max(scores, -1, keepdims=True)
    exponent = jnp.exp(scores - row_top)
    row_sum = jnp.sum(exponent, -1, keepdims=True)
    attn_prob = (exponent / row_sum).astype(jnp.bfloat16)
    attended = jnp.einsum(
        "fhpq,fqhe->fphe", attn_prob, values, preferred_element_type=jnp.float32
    ).astype(jnp.bfloat16)
    return (attended, (row_top + jnp.log(row_sum))[..., 0], queries, key_rows, values)


def spatial_backward(queries, key_rows, values, log_total, grad_out):
    scale_factor = queries.shape[-1] ** (-0.5)
    scores = (
        jnp.einsum("fphe,fqhe->fhpq", queries, key_rows, preferred_element_type=jnp.float32)
        * scale_factor
    )
    attn_prob = jnp.exp(scores - log_total[..., None])
    grad_prob = jnp.einsum("fphe,fqhe->fhpq", grad_out, values, preferred_element_type=jnp.float32)
    grad_values = jnp.einsum(
        "fhpq,fphe->fqhe",
        attn_prob.astype(jnp.bfloat16),
        grad_out,
        preferred_element_type=jnp.float32,
    )
    grad_scores = (
        attn_prob * (grad_prob - jnp.sum(attn_prob * grad_prob, -1, keepdims=True))
    ).astype(jnp.bfloat16)
    grad_queries = (
        jnp.einsum("fhpq,fqhe->fphe", grad_scores, key_rows, preferred_element_type=jnp.float32)
        * scale_factor
    )
    grad_keys = (
        jnp.einsum("fhpq,fphe->fqhe", grad_scores, queries, preferred_element_type=jnp.float32)
        * scale_factor
    )
    return (
        grad_queries.astype(jnp.bfloat16),
        grad_keys.astype(jnp.bfloat16),
        grad_values.astype(jnp.bfloat16),
    )


def temporal_scores(queries, key_rows, allowed):
    scale_factor = queries.shape[-1] ** (-0.5)
    scores = (
        jnp.einsum("gtphe,gsphe->gphts", queries, key_rows, preferred_element_type=jnp.float32)
        * scale_factor
    )
    return jnp.where(allowed[:, None, None], scores, -1000000000.0)


def temporal_forward(queries, key_rows, values, allowed):
    scores = temporal_scores(queries, key_rows, allowed)
    row_top = jnp.max(scores, -1, keepdims=True)
    exponent = jnp.exp(scores - row_top)
    row_sum = jnp.sum(exponent, -1, keepdims=True)
    attn_prob = (exponent / row_sum).astype(jnp.bfloat16)
    attended = jnp.einsum(
        "gphts,gsphe->gtphe", attn_prob, values, preferred_element_type=jnp.float32
    ).astype(jnp.bfloat16)
    return (attended, (row_top + jnp.log(row_sum))[..., 0])


def temporal_backward(queries, key_rows, values, log_total, grad_out, allowed):
    scale_factor = queries.shape[-1] ** (-0.5)
    scores = temporal_scores(queries, key_rows, allowed)
    attn_prob = jnp.exp(scores - log_total[..., None])
    grad_prob = jnp.einsum(
        "gtphe,gsphe->gphts", grad_out, values, preferred_element_type=jnp.float32
    )
    grad_values = jnp.einsum(
        "gphts,gtphe->gsphe",
        attn_prob.astype(jnp.bfloat16),
        grad_out,
        preferred_element_type=jnp.float32,
    )
    grad_scores = (
        attn_prob * (grad_prob - jnp.sum(attn_prob * grad_prob, -1, keepdims=True))
    ).astype(jnp.bfloat16)
    grad_queries = (
        jnp.einsum("gphts,gsphe->gtphe", grad_scores, key_rows, preferred_element_type=jnp.float32)
        * scale_factor
    )
    grad_keys = (
        jnp.einsum("gphts,gtphe->gsphe", grad_scores, queries, preferred_element_type=jnp.float32)
        * scale_factor
    )
    return (
        grad_queries.astype(jnp.bfloat16),
        grad_keys.astype(jnp.bfloat16),
        grad_values.astype(jnp.bfloat16),
    )


def block_forward(resid_in, gathered, block_idx, allowed):
    gain_pair, shift_pair, qkv_matrix, proj_matrix, in_matrix, in_bias, out_matrix = tuple(
        (array_item[block_idx] for array_item in gathered)
    )
    groups_n, steps_n, patches_n, model_width = resid_in.shape
    head_width = model_width // HEADS
    unit_one, inverse_one = norm_stats(resid_in)
    normed = (
        unit_one * gain_pair[0].astype(jnp.float32) + shift_pair[0].astype(jnp.float32)
    ).astype(jnp.bfloat16)
    mixed_qkv = apply_right(normed, qkv_matrix).astype(jnp.bfloat16)
    parts_qkv = mixed_qkv.reshape(groups_n, steps_n, patches_n, 3, HEADS, head_width)
    if block_idx == 0:
        frames = groups_n * steps_n
        pieces = tuple(
            (
                parts_qkv[:, :, :, part_idx].reshape(frames, patches_n, HEADS, head_width)
                for part_idx in range(3)
            )
        )
        attended, log_total, queries, key_rows, values = spatial_forward(
            (
                lax.all_to_all(pieces[0], "seq", split_axis=2, concat_axis=1, tiled=True),
                lax.all_to_all(pieces[1], "seq", split_axis=2, concat_axis=1, tiled=True),
                lax.all_to_all(pieces[2], "seq", split_axis=2, concat_axis=1, tiled=True),
            )
        )
        attended = lax.all_to_all(attended, "seq", split_axis=1, concat_axis=2, tiled=True)
    else:
        queries, key_rows, values = (
            parts_qkv[:, :, :, 0],
            parts_qkv[:, :, :, 1],
            parts_qkv[:, :, :, 2],
        )
        attended, log_total = temporal_forward(queries, key_rows, values, allowed)
    attended = attended.reshape(groups_n, steps_n, patches_n, model_width)
    middle = resid_in + apply_right(attended, proj_matrix)
    unit_two, inverse_two = norm_stats(middle)
    normed_two = (
        unit_two * gain_pair[1].astype(jnp.float32) + shift_pair[1].astype(jnp.float32)
    ).astype(jnp.bfloat16)
    pre_act = apply_right(normed_two, in_matrix) + in_bias.astype(jnp.float32)
    hidden = gelu_smooth(pre_act).astype(jnp.bfloat16)
    resid_out = middle + apply_right(hidden, out_matrix)
    kept_state = (
        unit_one,
        inverse_one,
        normed,
        queries,
        key_rows,
        values,
        log_total,
        attended,
        unit_two,
        inverse_two,
        normed_two,
        pre_act,
        hidden,
    )
    return (resid_out, kept_state)


def block_backward(grad_out, gathered, block_idx, allowed, kept_state):
    gain_pair, shift_pair, qkv_matrix, proj_matrix, in_matrix, in_bias, out_matrix = tuple(
        (array_item[block_idx] for array_item in gathered)
    )
    (
        unit_one,
        inverse_one,
        normed,
        queries,
        key_rows,
        values,
        log_total,
        attended,
        unit_two,
        inverse_two,
        normed_two,
        pre_act,
        hidden,
    ) = kept_state
    groups_n, steps_n, patches_n, model_width = grad_out.shape
    head_width = model_width // HEADS
    grad_branch = grad_out.astype(jnp.bfloat16)
    grad_hidden = apply_left(grad_branch, out_matrix)
    grad_pre = (grad_hidden * gelu_slope(pre_act)).astype(jnp.bfloat16)
    grad_b_in = row_total(grad_pre.astype(jnp.float32))
    grad_second = apply_left(grad_pre, in_matrix)
    gain_second = row_total(grad_second * unit_two)
    shift_second = row_total(grad_second)
    grad_middle = grad_out + norm_back(
        grad_second * gain_pair[1].astype(jnp.float32), unit_two, inverse_two
    )
    grad_proj_in = grad_middle.astype(jnp.bfloat16)
    grad_attended = apply_left(grad_proj_in, proj_matrix).astype(jnp.bfloat16)
    grad_split = grad_attended.reshape(groups_n, steps_n, patches_n, HEADS, head_width)
    if block_idx == 0:
        frames = groups_n * steps_n
        grad_heads = lax.all_to_all(
            grad_split.reshape(frames, patches_n, HEADS, head_width),
            "seq",
            split_axis=2,
            concat_axis=1,
            tiled=True,
        )
        grad_queries, grad_keys, grad_values = spatial_backward(
            queries, key_rows, values, log_total, grad_heads
        )
        grad_queries, grad_keys, grad_values = (
            lax.all_to_all(grad_queries, "seq", split_axis=1, concat_axis=2, tiled=True),
            lax.all_to_all(grad_keys, "seq", split_axis=1, concat_axis=2, tiled=True),
            lax.all_to_all(grad_values, "seq", split_axis=1, concat_axis=2, tiled=True),
        )
    else:
        grad_queries, grad_keys, grad_values = temporal_backward(
            queries, key_rows, values, log_total, grad_split, allowed
        )
    grad_mixed = jnp.stack(
        [
            array_item.reshape(groups_n, steps_n, patches_n, HEADS, head_width)
            for array_item in (grad_queries, grad_keys, grad_values)
        ],
        3,
    )
    grad_mixed = grad_mixed.reshape(groups_n, steps_n, patches_n, 3 * model_width)
    grad_first = apply_left(grad_mixed, qkv_matrix)
    gain_first = row_total(grad_first * unit_one)
    shift_first = row_total(grad_first)
    grad_input = grad_middle + norm_back(
        grad_first * gain_pair[0].astype(jnp.float32), unit_one, inverse_one
    )
    grad_gains = jnp.stack([gain_first, gain_second])
    grad_shifts = jnp.stack([shift_first, shift_second])
    pairs = (
        (normed, grad_mixed),
        (attended, grad_proj_in),
        (normed_two, grad_pre),
        (hidden, grad_branch),
    )
    return (grad_input, (grad_gains, grad_shifts, grad_b_in, pairs))


def joined_outer(results, pair_idx):
    left_rows = jnp.concatenate([result[3][pair_idx][0] for result in results], 1)
    right_rows = jnp.concatenate([result[3][pair_idx][1] for result in results], 1)
    return outer_sum(left_rows, right_rows)


def summed_small(results, member_idx):
    total = results[0][member_idx]
    for result in results[1:]:
        total = total + result[member_idx]
    return total


def on_device(tokens, lengths, cotangent, norm_gain, norm_bias, w_qkv, w_proj, w_in, b_in, w_out):
    steps_n = tokens.shape[1] // MICRO
    layer_n = w_qkv.shape[0] // 2
    mask_list = [clip_mask(lengths[:, micro_idx], steps_n) for micro_idx in range(MICRO)]
    states = [
        tokens[:, micro_idx * steps_n : (micro_idx + 1) * steps_n].astype(jnp.float32)
        for micro_idx in range(MICRO)
    ]
    stored = []
    layer_idx = 0
    gathered = (
        lax.all_gather(norm_gain, ("dp", "seq"), axis=2, tiled=True),
        lax.all_gather(norm_bias, ("dp", "seq"), axis=2, tiled=True),
        lax.all_gather(w_qkv, ("dp", "seq"), axis=1, tiled=True),
        lax.all_gather(w_proj, ("dp", "seq"), axis=1, tiled=True),
        lax.all_gather(w_in, ("dp", "seq"), axis=1, tiled=True),
        lax.all_gather(b_in, ("dp", "seq"), axis=1, tiled=True),
        lax.all_gather(w_out, ("dp", "seq"), axis=1, tiled=True),
    )
    stored.append(gathered)
    kept_micro = []
    for micro_idx in range(MICRO):
        kept_blocks = []
        for block_idx in range(2):
            states[micro_idx], kept_state = block_forward(
                states[micro_idx], gathered, block_idx, mask_list[micro_idx]
            )
            kept_blocks.append(kept_state)
        kept_micro.append(kept_blocks)
    kept_layers = [kept_micro]
    activations = jnp.concatenate(states, 1).astype(jnp.bfloat16)
    grad_states = [
        cotangent[:, micro_idx * steps_n : (micro_idx + 1) * steps_n].astype(jnp.float32)
        for micro_idx in range(MICRO)
    ]
    layer_sums = [None] * layer_n
    for layer_idx in reversed(range(layer_n)):
        gathered = (
            lax.all_gather(norm_gain, ("dp", "seq"), axis=2, tiled=True),
            lax.all_gather(norm_bias, ("dp", "seq"), axis=2, tiled=True),
            lax.all_gather(w_qkv, ("dp", "seq"), axis=1, tiled=True),
            lax.all_gather(w_proj, ("dp", "seq"), axis=1, tiled=True),
            lax.all_gather(w_in, ("dp", "seq"), axis=1, tiled=True),
            lax.all_gather(b_in, ("dp", "seq"), axis=1, tiled=True),
            lax.all_gather(w_out, ("dp", "seq"), axis=1, tiled=True),
        )
        block_sums = [None, None]
        for block_idx in (1, 0):
            results = []
            for micro_idx in range(MICRO):
                grad_states[micro_idx], block_result = block_backward(
                    grad_states[micro_idx],
                    gathered,
                    block_idx,
                    mask_list[micro_idx],
                    kept_layers[layer_idx][micro_idx][block_idx],
                )
                results.append(block_result)
            block_grads = (
                summed_small(results, 0),
                summed_small(results, 1),
                joined_outer(results, 0),
                joined_outer(results, 1),
                joined_outer(results, 2),
                summed_small(results, 2),
                joined_outer(results, 3),
            )
            block_sums[block_idx] = block_grads
        layer_sums[layer_idx] = tuple(
            (jnp.stack([block_sums[0][grad_idx], block_sums[1][grad_idx]]) for grad_idx in range(7))
        )
    merged = tuple((layer_sums[0][grad_idx] for grad_idx in range(7)))
    merged = (
        lax.psum_scatter(merged[0], ("dp", "seq"), scatter_dimension=2, tiled=True),
        lax.psum_scatter(merged[1], ("dp", "seq"), scatter_dimension=2, tiled=True),
        lax.psum_scatter(merged[2], ("dp", "seq"), scatter_dimension=1, tiled=True),
        lax.psum_scatter(merged[3], ("dp", "seq"), scatter_dimension=1, tiled=True),
        lax.psum_scatter(merged[4], ("dp", "seq"), scatter_dimension=1, tiled=True),
        lax.psum_scatter(merged[5], ("dp", "seq"), scatter_dimension=1, tiled=True),
        lax.psum_scatter(merged[6], ("dp", "seq"), scatter_dimension=1, tiled=True),
    )
    grad_tokens = jnp.concatenate(grad_states, 1).astype(jnp.bfloat16)
    return (
        activations,
        grad_tokens,
        merged[0],
        merged[1],
        merged[2],
        merged[3],
        merged[4],
        merged[5],
        merged[6],
    )


def solution(mesh):
    in_specs = (
        P("dp", None, "seq", None),
        P("dp", None, None),
        P("dp", None, "seq", None),
        P(None, None, ("dp", "seq")),
        P(None, None, ("dp", "seq")),
        P(None, ("dp", "seq"), None),
        P(None, ("dp", "seq"), None),
        P(None, ("dp", "seq"), None),
        P(None, ("dp", "seq")),
        P(None, ("dp", "seq"), None),
    )
    out_specs = (
        P("dp", None, "seq", None),
        P("dp", None, "seq", None),
        P(None, None, ("dp", "seq")),
        P(None, None, ("dp", "seq")),
        P(None, ("dp", "seq"), None),
        P(None, ("dp", "seq"), None),
        P(None, ("dp", "seq"), None),
        P(None, ("dp", "seq")),
        P(None, ("dp", "seq"), None),
    )
    return jax.shard_map(
        on_device, mesh=mesh, in_specs=in_specs, out_specs=out_specs, check_vma=False
    )
```

profile of v0, /device:TPU:0, one launch (start us, length us, event | category | flops | bytes accessed | tf_op | source)
XLA Modules:
  0.0 1885.0 jit_solution(15987239503384712537)
XLA Ops:
  11.0 71.6 %all_gather.26 = bf16[2,2,512]{1,0,2:T(2,128)(2,1)S(1)} all-gather(bf16[2,2,16]{1,0,2:T(2,128)(2,1)S(1)} %copy.417), channel_id=1, replica_groups=mesh['dp'=16,'seq'=2] {'dp','seq'}, dimensions={2}, use_global_device_ids=true | all-gather | bytes 4224 | tf_op jit(solution)/shard_map/all_gather | solution.py:327
  82.6 65.3 %all_gather.27 = bf16[2,2,512]{1,0,2:T(2,128)(2,1)S(1)} all-gather(bf16[2,2,16]{1,0,2:T(2,128)(2,1)S(1)} %copy.418), channel_id=1, replica_groups=mesh['dp'=16,'seq'=2] {'dp','seq'}, dimensions={2}, use_global_device_ids=true | all-gather | bytes 4224 | tf_op jit(solution)/shard_map/all_gather | solution.py:328
  150.8 5.7 fusion.234
  156.6 6.2 fusion.233
  165.0 5.2 convolution_convert_fusion.1
  170.2 4.7 copy.440
  186.7 8.5 all-to-all-done.5
  199.7 74.1 %all-gather = bf16[32,64,2]{1,2,0:T(2,128)(2,1)S(1)} all-gather(bf16[1,64,2]{1,2,0:T(2,128)(2,1)S(1)} %bitcast.801), channel_id=1, replica_groups=mesh['dp'=16,'seq'=2] {'dp','seq'}, dimensions={0}, use_global_device_ids=true | all-gather | bytes 8448 | tf_op jit(solution)/shard_map/all_gather | solution.py:332
  281.4 5.2 convolution_convert_fusion.3
  286.5 4.7 copy.419
  320.2 5.8 multiply_reduce_fusion.2
  326.0 4.6 all-to-all-start.2
  330.7 4.9 fusion.39
  335.5 6.3 all-to-all-done.2
  346.3 6.2 fusion.190
  403.2 6.2 copy.551
  414.2 5.0 copy.550
  428.0 4.7 fusion.199
  436.0 8.3 multiply_convert_fusion.5
  444.2 6.0 fusion.294
  461.8 4.7 copy.452
  470.7 4.7 copy.568
  475.3 4.7 copy.569
  480.0 5.6 fusion.141
  491.3 4.5 copy.457
  499.4 4.9 convert_bitcast_fusion.2
  529.0 4.9 fusion.151
  547.1 5.0 convert_bitcast_fusion.3
  566.0 8.3 multiply_convert_fusion.4
  574.3 6.2 convert_reduce_fusion
  580.5 9.7 convert_reduce_fusion.1
  608.3 5.6 fusion.145
  622.1 4.7 fusion.169
  636.5 5.6 fusion.155
  657.2 4.5 copy.493
  669.0 8.9 copy.494
  689.4 8.9 copy.468
  714.5 8.8 convert_reduce_fusion.2
  725.8 5.6 convert_reduce_fusion.3
  757.6 4.6 all-to-all-start.12
  766.0 5.5 multiply_reduce_fusion.1
  783.7 4.5 fusion.192
  798.3 4.9 fusion.186
  814.8 6.5 multiply_reduce_fusion
  828.6 6.9 multiply_convert_fusion
  845.1 4.6 all-to-all-start.13
  851.2 4.5 fusion.194
  865.9 5.0 fusion.183
  946.6 4.9 copy.518
  951.5 4.7 copy.517
  956.1 8.7 fusion.58
  967.6 4.9 copy.513
  972.5 6.2 fusion.59
  983.4 7.7 fusion.61
  991.1 4.6 fusion.60
  1001.6 7.3 fusion.63
  1008.9 4.6 fusion.62
  1019.0 5.3 fusion.149
  1036.0 86.6 %reduce-scatter.24.cloned.1.call-done = f32[16,4]{1,0:T(8,128)} async-done(((f32[512,4]{1,0:T(8,128)}), f32[16,4]{1,0:T(8,128)}) %reduce-scatter.24.cloned.1.call-update) | async-done | bytes 272
  1124.0 130.1 %reduce-scatter.22.cloned.1.call-done = f32[16,4]{1,0:T(8,128)} async-done(((f32[512,4]{1,0:T(8,128)}), f32[16,4]{1,0:T(8,128)}) %reduce-scatter.22.cloned.1.call-update) | async-done | bytes 272
  1255.5 134.3 %reduce-scatter.16.cloned.1.call-done = f32[2,16,512]{2,1,0:T(8,128)} async-done(((f32[2,512,512]{2,1,0:T(8,128)}), f32[2,16,512]{2,1,0:T(8,128)}) %reduce-scatter.16.cloned.1.call-update) | async-done | bytes 65552 | tf_op jit(solution)/shard_map/reduce_scatter | solution.py:392
  1389.8 116.9 %reduce-scatter.14.cloned.1.call-done = f32[2,16,1536]{2,1,0:T(8,128)} async-done(((f32[2,512,1536]{2,1,0:T(8,128)}), f32[2,16,1536]{2,1,0:T(8,128)}) %reduce-scatter.14.cloned.1.call-update) | async-done | bytes 196624 | tf_op jit(solution)/shard_map/reduce_scatter | solution.py:391
  1506.7 185.1 %reduce-scatter.20.cloned.1.call-done = f32[2,64,512]{2,1,0:T(8,128)} async-done(((f32[2,2048,512]{2,1,0:T(8,128)}), f32[2,64,512]{2,1,0:T(8,128)}) %reduce-scatter.20.cloned.1.call-update) | async-done | bytes 262160 | tf_op jit(solution)/shard_map/reduce_scatter | solution.py:395
  1691.9 186.5 %reduce-scatter.18.cloned.1.call-done = f32[2,16,2048]{2,1,0:T(8,128)} async-done(((f32[2,512,2048]{2,1,0:T(8,128)}), f32[2,16,2048]{2,1,0:T(8,128)}) %reduce-scatter.18.cloned.1.call-update) | async-done | bytes 262160 | tf_op jit(solution)/shard_map/reduce_scatter | solution.py:393
  (658 shorter events, 498.0 us)
Async XLA Ops:
  7.2 142.7 %copy-start.7 = (bf16[1,16,128,512]{3,2,1,0:T(8,128)(2,1)S(1)}, bf16[1,16,128,512]{3,2,1,0:T(8,128)(2,1)}, u32[]{:S(2)}) copy-start(bf16[1,16,128,512]{3,2,1,0:T(8,128)(2,1)} %param.10) | copy-start | bytes 6291460
  7.2 157.8 %all-gather.6.cloned.1.call-start = ((), (), s32[]{:S(2)}) async-start(), calls=%async_computation.23 | async-start | bytes 3244032 | tf_op jit(solution)/shard_map/all_gather | solution.py:329
  7.9 412.5 %all-gather.8.cloned.1.call-start = ((), (), s32[]{:S(2)}) async-start(), calls=%async_computation.24 | async-start | bytes 1081344 | tf_op jit(solution)/shard_map/all_gather | solution.py:330
  8.7 419.3 %all-gather.10.cloned.1.call-start = ((), (), s32[]{:S(2)}) async-start(), calls=%async_computation.25 | async-start | bytes 4325376 | tf_op jit(solution)/shard_map/all_gather | solution.py:331
  149.8 12.9 copy-start.107
  149.8 12.9 copy-start.109
  150.8 14.1 copy-start.127
  150.8 14.1 copy-start.129
  156.6 8.4 copy-start.143
  156.6 269.7 %copy-start.125 = (f32[512]{0:T(512)}, f32[512]{0:T(512)S(1)}, u32[]{:S(2)}) copy-start(f32[512]{0:T(512)S(1)} %get-tuple-element.49) | copy-start | bytes 6148
  156.6 298.9 %copy-start.123 = (f32[512]{0:T(512)}, f32[512]{0:T(512)S(1)}, u32[]{:S(2)}) copy-start(f32[512]{0:T(512)S(1)} %get-tuple-element.48) | copy-start | bytes 6148
  179.9 15.2 all-to-all-start.5
  183.5 260.7 %all-gather.12.cloned.1.call-start = ((), (), s32[]{:S(2)}) async-start(), calls=%async_computation.26 | async-start | bytes 4325376 | tf_op jit(solution)/shard_map/all_gather | solution.py:333
  184.4 15.3 copy-start.160
  195.2 81.8 %all-to-all-start.6 = ((bf16[8,128,8,64]{1,3,0,2:T(8,128)(2,1)}), bf16[8,128,8,64]{1,3,0,2:T(8,128)(2,1)}, u32[]{:S(2)}, u32[]{:S(2)}) async-start(bf16[8,128,8,64]{1,3,0,2:T(8,128)(2,1)} %copy.445), calls=%async_computation.6 | async-start | bytes 2097152 | tf_op jit(solution)/shard_map/all_to_all | solution.py:184
  199.7 289.9 %copy-start.145 = (pred[8,8]{1,0:T(8,128)(4,1)}, pred[8,8]{1,0:T(8,128)(4,1)S(1)}, u32[]{:S(2)}) copy-start(pred[8,8]{1,0:T(8,128)(4,1)S(1)} %fusion.251) | copy-start | bytes 196
  274.6 158.1 %copy-start.154 = (f32[1,2048]{1,0:T(1,128)}, f32[1,2048]{1,0:T(1,128)S(1)}, u32[]{:S(2)}) copy-start(f32[1,2048]{1,0:T(1,128)S(1)} %get-tuple-element.90) | copy-start | bytes 24580
  276.9 19.4 %all-to-all-start.4 = ((bf16[8,128,8,64]{1,3,0,2:T(8,128)(2,1)}), bf16[8,128,8,64]{1,3,0,2:T(8,128)(2,1)}, u32[]{:S(2)}, u32[]{:S(2)}) async-start(bf16[8,128,8,64]{1,3,0,2:T(8,128)(2,1)} %copy.441), calls=%async_computation.4 | async-start | bytes 2097152 | tf_op jit(solution)/shard_map/all_to_all | solution.py:185
  296.4 29.7 %all-to-all-start.1 = ((bf16[8,128,8,64]{1,3,0,2:T(8,128)(2,1)}), bf16[8,128,8,64]{1,3,0,2:T(8,128)(2,1)}, u32[]{:S(2)}, u32[]{:S(2)}) async-start(bf16[8,128,8,64]{1,3,0,2:T(8,128)(2,1)} %copy.422), calls=%async_computation.1 | async-start | bytes 2097152 | tf_op jit(solution)/shard_map/all_to_all | solution.py:183
  326.0 15.8 all-to-all-start.2
  335.5 10.8 copy-start.53
  341.9 27.4 %all-to-all-start = ((bf16[8,128,8,64]{1,3,0,2:T(8,128)(2,1)}), bf16[8,128,8,64]{1,3,0,2:T(8,128)(2,1)}, u32[]{:S(2)}, u32[]{:S(2)}) async-start(bf16[8,128,8,64]{1,3,0,2:T(8,128)(2,1)} %copy.420), calls=%async_computation | async-start | bytes 2097152 | tf_op jit(solution)/shard_map/all_to_all | solution.py:185
  369.2 10.2 copy-start.34
  369.3 24.5 %all-to-all-start.7 = ((bf16[2,2,131072]{2,1,0:T(2,128)(2,1)}), bf16[2,2,131072]{2,1,0:T(2,128)(2,1)}, u32[]{:S(2)}, u32[]{:S(2)}) async-start(bf16[2,2,131072]{2,1,0:T(2,128)(2,1)} %reshape.1644), calls=%async_computation.7 | async-start | bytes 2097152 | tf_op jit(solution)/shard_map/all_to_all | solution.py:188
  393.7 18.2 all-to-all-start.3
  428.0 8.0 copy-start.165
  450.2 57.5 %copy-start.5 = (f32[1,8,128,512]{3,2,1,0:T(8,128)}, f32[1,8,128,512]{3,2,1,0:T(8,128)S(1)}, u32[]{:S(2)}) copy-start(f32[1,8,128,512]{3,2,1,0:T(8,128)S(1)} %get-tuple-element.125) | copy-start | bytes 6291460
  525.3 8.7 copy-start.24
  537.8 9.3 copy-start.59
  538.1 8.9 copy-start.103
  558.3 148.0 %copy-start.3 = (f32[1,8,128,512]{3,2,1,0:T(8,128)}, f32[1,8,128,512]{3,2,1,0:T(8,128)S(1)}, u32[]{:S(2)}) copy-start(f32[1,8,128,512]{3,2,1,0:T(8,128)S(1)} %get-tuple-element.127) | copy-start | bytes 6291460
  558.8 38.6 %copy-start.121 = (f32[8,128]{1,0:T(8,128)}, f32[8,128]{1,0:T(8,128)S(1)}, u32[]{:S(2)}) copy-start(f32[8,128]{1,0:T(8,128)S(1)} %add_rsqrt_fusion.4) | copy-start | bytes 12292
  566.0 8.3 copy-start.40
  566.0 8.3 copy-start.162
  580.5 9.7 copy-start.176
  669.0 8.9 copy-start.100
  711.1 14.6 copy-start.78
  711.2 14.5 slice-start.2
  714.1 9.2 copy-start.80
  714.5 8.8 copy-start.167
  714.5 11.2 slice-start.3
  725.7 9.1 copy-start.31
  743.8 13.8 all-to-all-start.8
  757.6 36.3 %all-to-all-start.12 = ((bf16[8,128,8,64]{1,3,0,2:T(8,128)(2,1)}), bf16[8,128,8,64]{1,3,0,2:T(8,128)(2,1)}, u32[]{:S(2)}, u32[]{:S(2)}) async-start(bf16[8,128,8,64]{1,3,0,2:T(8,128)(2,1)} %copy.497), calls=%async_computation.12 | async-start | bytes 2097152 | tf_op jit(solution)/shard_map/all_to_all | solution.py:259
  793.9 16.9 all-to-all-start.9
  810.8 13.4 all-to-all-start.10
  824.1 11.4 copy-start.57
  824.1 21.0 %all-to-all-start.11 = ((bf16[2,2,131072]{2,1,0:T(2,128)(2,1)}), bf16[2,2,131072]{2,1,0:T(2,128)(2,1)}, u32[]{:S(2)}, u32[]{:S(2)}) async-start(bf16[2,2,131072]{2,1,0:T(2,128)(2,1)} %reshape.1654), calls=%async_computation.11 | async-start | bytes 2097152 | tf_op jit(solution)/shard_map/all_to_all | solution.py:272
  828.6 9.0 copy-start.33
  845.1 16.3 all-to-all-start.13
  849.7 179.1 %reduce-scatter.26.cloned.1.call-start = ((), (), s32[]{:S(2)}) async-start(), calls=%async_computation.33 | async-start | bytes 1081344
  861.4 15.3 all-to-all-start.14
  872.8 8.6 copy-start.157
  872.8 8.6 copy-start.158
  872.8 8.6 copy-start.62
  876.7 42.5 %all-to-all-start.15 = ((bf16[2,2,131072]{2,1,0:T(2,128)(2,1)}), bf16[2,2,131072]{2,1,0:T(2,128)(2,1)}, u32[]{:S(2)}, u32[]{:S(2)}) async-start(bf16[2,2,131072]{2,1,0:T(2,128)(2,1)} %reshape.1648), calls=%async_computation.15 | async-start | bytes 2097152 | tf_op jit(solution)/shard_map/all_to_all | solution.py:272
  881.2 241.4 %reduce-scatter.24.cloned.1.call-start = ((), (), s32[]{:S(2)}) async-start(), calls=%async_computation.32 | async-start | bytes 270336
  940.1 314.0 %reduce-scatter.22.cloned.1.call-start = ((), (), s32[]{:S(2)}) async-start(), calls=%async_computation.31 | async-start | bytes 270336
  943.3 446.5 %reduce-scatter.16.cloned.1.call-start = ((), (), s32[]{:S(2)}) async-start(), calls=%async_computation.28 | async-start | bytes 2162688 | tf_op jit(solution)/shard_map/reduce_scatter | solution.py:392
  946.5 560.2 %reduce-scatter.14.cloned.1.call-start = ((), (), s32[]{:S(2)}) async-start(), calls=%async_computation.27 | async-start | bytes 6488064 | tf_op jit(solution)/shard_map/reduce_scatter | solution.py:391
  981.9 710.0 %reduce-scatter.20.cloned.1.call-start = ((), (), s32[]{:S(2)}) async-start(), calls=%async_computation.30 | async-start | bytes 8650752 | tf_op jit(solution)/shard_map/reduce_scatter | solution.py:395
  983.4 7.7 copy-start.173
  983.4 7.7 copy-start.175
  1000.0 878.3 %reduce-scatter.18.cloned.1.call-start = ((), (), s32[]{:S(2)}) async-start(), calls=%async_computation.29 | async-start | bytes 8650752 | tf_op jit(solution)/shard_map/reduce_scatter | solution.py:393
  (150 other events, 519.8 us)
Sparse Core Ops, SparseCore 0:
  11.0 62.1 all-gather.5
  76.2 52.7 all-gather.7
  132.1 65.9 all-gather.9
  201.0 61.8 all-gather.11
  852.4 138.1 reduce-scatter.25
  992.8 129.6 reduce-scatter.23
  1124.7 129.3 reduce-scatter.21
  1257.0 132.7 reduce-scatter.15
  1396.0 110.6 reduce-scatter.13
  1509.5 182.2 reduce-scatter.19
  1694.8 183.4 reduce-scatter.17
where the time goes:
time: 1900 us; the launch traced here: 1890 us
  waiting for transfers between devices  864 us (45%)
  local copies, waits for them, and re-layouts  357 us (19%)
  matrix products  272 us (14%)
  blocking collectives  211 us (11%)
  other arithmetic  94.6 us (5%)
  starting transfers between devices  69.3 us (4%)
    unnamed x14, waiting for transfers between devices  219 us
    reduce_scatter x1, waiting for transfers between devices, on_device(): lax.psum_scatter(merged[4], ('dp', 'seq'), scatter_dimension=1, tiled=True)  186 us
    reduce_scatter x1, waiting for transfers between devices, on_device(): lax.psum_scatter(merged[6], ('dp', 'seq'), scatter_dimension=1, tiled=True)  185 us
    reduce_scatter x1, waiting for transfers between devices, on_device(): lax.psum_scatter(merged[3], ('dp', 'seq'), scatter_dimension=1, tiled=True)  134 us
    unnamed x409, local copies, waits for them, and re-layouts  119 us
    reduce_scatter x1, waiting for transfers between devices, on_device(): lax.psum_scatter(merged[2], ('dp', 'seq'), scatter_dimension=1, tiled=True)  117 us
    all_gather x1, blocking collectives, on_device(): lax.all_gather(b_in, ('dp', 'seq'), axis=1, tiled=True)  74.1 us
    all_gather x1, blocking collectives, on_device(): lax.all_gather(norm_gain, ('dp', 'seq'), axis=2, tiled=True)  71.6 us
  transfers between devices with their start and end apart: 27, of which 11 were waited for; matrix products, arithmetic and copies ran while one was open for 21% of the time, Pallas kernels for 0%

commit v1 on v0

v1 whole, which is shorter than its diff:
```python
import functools

import jax
import jax.numpy as jnp
from jax import lax
from jax.experimental import pallas as pl
from jax.experimental.pallas import tpu as pltpu
from jax.sharding import PartitionSpec as P

HEADS = 8
MICRO = 2
LANES = 128
AXES = ("dp", "seq")
BF = jnp.bfloat16
F32 = jnp.float32
MIB = 1 << 20
FROM_A, FROM_B, TO_A, TO_B = range(4)


def dot(left, right, left_dim, right_dim):
    return lax.dot_general(
        left, right, (((left_dim,), (right_dim,)), ((), ())), preferred_element_type=F32
    )


def norm_stats(values):
    centre = values - jnp.mean(values, -1, keepdims=True)
    variance = jnp.mean(centre * centre, -1, keepdims=True)
    inverse = lax.rsqrt(variance + 1e-05)
    return centre * inverse, inverse


def norm_back(grad_scaled, unit_rows, inverse):
    mean_grad = jnp.mean(grad_scaled, -1, keepdims=True)
    mean_cross = jnp.mean(grad_scaled * unit_rows, -1, keepdims=True)
    return inverse * (grad_scaled - mean_grad - unit_rows * mean_cross)


def fold_rows(values):
    return jnp.sum(values.reshape(-1, 8, values.shape[-1]), 0)


def gelu_pair(values):
    cumulative = 0.5 * (1.0 + lax.erf(values * 0.7071067811865476))
    slope = cumulative + values * jnp.exp(-0.5 * values * values) * 0.3989422804014327
    return values * cumulative, slope


def start_weight(pieces, table_ref, which, held, sem):
    slab = 0
    for piece in pieces:
        rows = piece.shape[1]
        for idx in range(piece.shape[0]):
            first = pl.multiple_of(table_ref[which, slab] * rows, rows)
            pltpu.make_async_copy(piece.at[idx], held.at[pl.ds(first, rows)], sem).start()
            slab += 1


def wait_weight(held, sem):
    pltpu.make_async_copy(held, held, sem).wait()


def start_slabs(staged, table_ref, which, out, sem):
    rows = out.shape[1]
    for idx in range(out.shape[0]):
        first = pl.multiple_of(table_ref[which, idx] * rows, rows)
        pltpu.make_async_copy(staged.at[pl.ds(first, rows)], out.at[idx], sem).start()


def wait_slabs(out, sem):
    pltpu.make_async_copy(out, out, sem).wait()


def head_rows(head, width, value):
    lane = lax.broadcasted_iota(jnp.int32, (1, LANES), 1)
    inside = (lane >= head * width) & (lane < (head + 1) * width)
    return jnp.where(inside, value, 0.0).astype(BF)


def merge_heads(parts, width):
    lane = lax.broadcasted_iota(jnp.int32, (1, LANES), 1)
    merged = parts[-1]
    for head in range(len(parts) - 2, -1, -1):
        merged = jnp.where(lane < (head + 1) * width, parts[head], merged)
    return merged


def attend_forward(load, model, store, keep, bias):
    width = model // HEADS
    each = LANES // width
    scale = width ** (-0.5)
    for pair in range(model // LANES):
        first = pair * LANES
        queries = load(first)
        key_rows = load(model + first)
        values = load(2 * model + first)
        parts = []
        for sub in range(each):
            scores = dot(key_rows, queries * head_rows(sub, width, scale), 1, 1)
            if bias is not None:
                scores = scores + bias
            exponent = jnp.exp(scores - jnp.max(scores, 0, keepdims=True))
            prob = (exponent * (1.0 / jnp.sum(exponent, 0, keepdims=True))).astype(BF)
            keep(pair * each + sub, prob)
            parts.append(dot(prob, values, 0, 0))
        store(first, merge_heads(parts, width).astype(BF))


def attend_backward(load, load_grad, load_prob, model, store):
    width = model // HEADS
    each = LANES // width
    scale = width ** (-0.5)
    for pair in range(model // LANES):
        first = pair * LANES
        queries = load(first)
        key_rows = load(model + first)
        values = load(2 * model + first)
        grad_out = load_grad(first)
        scaled_q = queries * jnp.asarray(scale, BF)
        scaled_k = key_rows * jnp.asarray(scale, BF)
        grad_q, grad_k, grad_v = [], [], []
        for sub in range(each):
            prob = load_prob(pair * each + sub)
            grad_prob = dot(values, grad_out * head_rows(sub, width, 1.0), 1, 1)
            prob_wide = prob.astype(F32)
            total = jnp.sum(prob_wide * grad_prob, 0, keepdims=True)
            grad_scores = (prob_wide * (grad_prob - total)).astype(BF)
            grad_v.append(dot(prob, grad_out, 1, 0))
            grad_k.append(dot(grad_scores, scaled_q, 1, 0))
            grad_q.append(dot(grad_scores, scaled_k, 0, 0))
        store(first, merge_heads(grad_q, width).astype(BF))
        store(model + first, merge_heads(grad_k, width).astype(BF))
        store(2 * model + first, merge_heads(grad_v, width).astype(BF))


def spatial_forward_kernel(counts, table_ref, *refs):
    n_qkv, n_proj = counts
    qkv_pieces, refs = refs[:n_qkv], refs[n_qkv:]
    proj_pieces, refs = refs[:n_proj], refs[n_proj:]
    (
        own_ref,
        other_ref,
        vec_ref,
        middle_ref,
        qkv_ref,
        attended_ref,
        prob_ref,
        w_qkv,
        w_proj,
        sems,
    ) = refs
    frames, half, model = own_ref.shape

    @pl.when(pl.program_id(0) == 0)
    def _():
        start_weight(qkv_pieces, table_ref, FROM_A, w_qkv, sems.at[0])
        start_weight(proj_pieces, table_ref, FROM_A, w_proj, sems.at[1])
        wait_weight(w_qkv, sems.at[0])
        wait_weight(w_proj, sems.at[1])

    rows = jnp.concatenate([own_ref[...], other_ref[...]], 1).astype(F32)
    rows = rows.reshape(frames * 2 * half, model)
    unit, _ = norm_stats(rows)
    normed = (unit * vec_ref[0:1] + vec_ref[1:2]).astype(BF)
    qkv_ref[...] = dot(normed, w_qkv[...], 1, 0).astype(BF).reshape(qkv_ref.shape)
    for frame in range(frames):

        def load(first):
            return qkv_ref[frame, :, first : first + LANES]

        def store(first, value):
            attended_ref[frame, :, first : first + LANES] = value

        def keep(head, value):
            prob_ref[frame, head] = value

        attend_forward(load, model, store, keep, None)
    attended = attended_ref[...].reshape(rows.shape)
    middle = rows + dot(attended, w_proj[...], 1, 0)
    middle_ref[...] = middle.reshape(middle_ref.shape)


def feed_forward_kernel(counts, table_ref, *refs):
    n_in, n_out = counts
    in_pieces, refs = refs[:n_in], refs[n_in:]
    out_pieces, refs = refs[:n_out], refs[n_out:]
    (
        middle_ref,
        vec_ref,
        b_in_ref,
        result_ref,
        hidden_ref,
        slope_ref,
        w_in,
        w_out,
        sems,
    ) = refs

    @pl.when(pl.program_id(0) == 0)
    def _():
        start_weight(in_pieces, table_ref, FROM_A, w_in, sems.at[0])
        start_weight(out_pieces, table_ref, FROM_B, w_out, sems.at[1])
        wait_weight(w_in, sems.at[0])
        wait_weight(w_out, sems.at[1])

    middle = middle_ref[...]
    unit, _ = norm_stats(middle)
    normed = (unit * vec_ref[2:3] + vec_ref[3:4]).astype(BF)
    result_ref[...] = middle + ff_through(normed, b_in_ref, w_in, w_out, hidden_ref, slope_ref)


def ff_through(normed, b_in_ref, w_in, w_out, hidden_ref, slope_ref):
    width = w_in.shape[1]
    chunk = min(512, width)
    total = None
    for first in range(0, width, chunk):
        cols = slice(first, first + chunk)
        pre_act = dot(normed, w_in[:, cols], 1, 0) + b_in_ref[:, cols]
        hidden, slope = gelu_pair(pre_act)
        hidden = hidden.astype(BF)
        hidden_ref[:, cols] = hidden
        slope_ref[:, cols] = slope.astype(BF)
        term = dot(hidden, w_out[cols, :], 1, 0)
        total = term if total is None else total + term
    return total


def ff_back(grad_out, normed, unit, inverse, gain, w_in, w_out, hidden_ref, slope_ref, sums):
    acc_in, acc_out, small_ref = sums
    model, width = w_in.shape
    chunk = min(512, width)
    branch = grad_out.astype(BF)
    grad_second = None
    for first in range(0, width, chunk):
        cols = slice(first, first + chunk)
        grad_hidden = dot(branch, w_out[cols, :], 1, 1)
        grad_pre = (grad_hidden * slope_ref[:, cols].astype(F32)).astype(BF)
        small_ref[:, 2 * model + first : 2 * model + first + chunk] += fold_rows(
            grad_pre.astype(F32)
        )
        acc_out[cols, :] += dot(hidden_ref[:, cols], branch, 0, 0)
        acc_in[:, cols] += dot(normed, grad_pre, 0, 0)
        term = dot(grad_pre, w_in[:, cols], 1, 1)
        grad_second = term if grad_second is None else grad_second + term
    small_ref[:, :model] += fold_rows(grad_second * unit)
    small_ref[:, model : 2 * model] += fold_rows(grad_second)
    return grad_out + norm_back(grad_second * gain, unit, inverse)


def feed_backward_kernel(counts, table_ref, *refs):
    n_in, n_out = counts
    in_pieces, refs = refs[:n_in], refs[n_in:]
    out_pieces, refs = refs[:n_out], refs[n_out:]
    (
        grad_ref,
        middle_ref,
        hidden_ref,
        slope_ref,
        vec_ref,
        grad_middle_ref,
        small_ref,
        grad_in_out,
        grad_out_out,
        w_in,
        w_out,
        acc_in,
        acc_out,
        sems,
    ) = refs

    @pl.when(pl.program_id(0) == 0)
    def _():
        start_weight(in_pieces, table_ref, FROM_A, w_in, sems.at[0])
        start_weight(out_pieces, table_ref, FROM_B, w_out, sems.at[1])
        acc_in[...] = jnp.zeros_like(acc_in)
        acc_out[...] = jnp.zeros_like(acc_out)
        small_ref[...] = jnp.zeros_like(small_ref)
        wait_weight(w_in, sems.at[0])
        wait_weight(w_out, sems.at[1])

    unit, inverse = norm_stats(middle_ref[...])
    normed = (unit * vec_ref[2:3] + vec_ref[3:4]).astype(BF)
    grad_middle_ref[...] = ff_back(
        grad_ref[...],
        normed,
        unit,
        inverse,
        vec_ref[2:3],
        w_in,
        w_out,
        hidden_ref,
        slope_ref,
        (acc_in, acc_out, small_ref),
    )

    @pl.when(pl.program_id(0) == pl.num_programs(0) - 1)
    def _():
        w_out[...] = acc_out[...].astype(BF)
        start_slabs(w_out, table_ref, TO_B, grad_out_out, sems.at[1])
        w_in[...] = acc_in[...].astype(BF)
        start_slabs(w_in, table_ref, TO_A, grad_in_out, sems.at[0])
        wait_slabs(grad_out_out, sems.at[1])
        wait_slabs(grad_in_out, sems.at[0])


def spatial_backward_kernel(counts, table_ref, *refs):
    n_qkv, n_proj = counts
    qkv_pieces, refs = refs[:n_qkv], refs[n_qkv:]
    proj_pieces, refs = refs[:n_proj], refs[n_proj:]
    (
        grad_ref,
        own_ref,
        other_ref,
        qkv_ref,
        attended_ref,
        prob_ref,
        vec_ref,
        grad_own_ref,
        grad_other_ref,
        small_ref,
        grad_qkv_out,
        grad_proj_out,
        w_qkv,
        w_proj,
        acc_qkv,
        acc_proj,
        grad_att,
        grad_mixed,
        sems,
    ) = refs
    frames, half, model = own_ref.shape

    @pl.when(pl.program_id(0) == 0)
    def _():
        start_weight(qkv_pieces, table_ref, FROM_A, w_qkv, sems.at[0])
        start_weight(proj_pieces, table_ref, FROM_A, w_proj, sems.at[1])
        acc_qkv[...] = jnp.zeros_like(acc_qkv)
        acc_proj[...] = jnp.zeros_like(acc_proj)
        small_ref[...] = jnp.zeros_like(small_ref)
        wait_weight(w_qkv, sems.at[0])
        wait_weight(w_proj, sems.at[1])

    rows = jnp.concatenate([own_ref[...], other_ref[...]], 1).astype(F32)
    rows = rows.reshape(frames * 2 * half, model)
    unit, inverse = norm_stats(rows)
    normed = (unit * vec_ref[0:1] + vec_ref[1:2]).astype(BF)
    grad_middle = grad_ref[...].reshape(rows.shape)
    proj_in = grad_middle.astype(BF)
    acc_proj[...] += dot(attended_ref[...].reshape(rows.shape), proj_in, 0, 0)
    grad_att[...] = dot(proj_in, w_proj[...], 1, 1).astype(BF)
    for frame in range(frames):
        frame_rows = slice(frame * 2 * half, (frame + 1) * 2 * half)

        def load(first):
            return qkv_ref[frame, :, first : first + LANES]

        def load_grad(first):
            return grad_att[frame_rows, first : first + LANES]

        def load_prob(head):
            return prob_ref[frame, head]

        def store(first, value):
            grad_mixed[frame_rows, first : first + LANES] = value

        attend_backward(load, load_grad, load_prob, model, store)
    acc_qkv[...] += dot(normed, grad_mixed[...], 0, 0)
    grad_first = dot(grad_mixed[...], w_qkv[...], 1, 1)
    small_ref[:, :model] += fold_rows(grad_first * unit)
    small_ref[:, model : 2 * model] += fold_rows(grad_first)
    grad_rows = grad_middle + norm_back(grad_first * vec_ref[0:1], unit, inverse)
    grad_rows = grad_rows.astype(BF).reshape(frames, 2 * half, model)
    grad_own_ref[...] = grad_rows[:, :half]
    grad_other_ref[...] = grad_rows[:, half:]

    @pl.when(pl.program_id(0) == pl.num_programs(0) - 1)
    def _():
        w_qkv[...] = acc_qkv[...].astype(BF)
        start_slabs(w_qkv, table_ref, TO_A, grad_qkv_out, sems.at[0])
        w_proj[...] = acc_proj[...].astype(BF)
        start_slabs(w_proj, table_ref, TO_A, grad_proj_out, sems.at[1])
        wait_slabs(grad_qkv_out, sems.at[0])
        wait_slabs(grad_proj_out, sems.at[1])


def temporal_kernel(counts, tile, table_ref, *refs):
    groups = []
    for count in counts:
        groups.append(refs[:count])
        refs = refs[count:]
    (
        rows_ref,
        own_ref,
        other_ref,
        vec_ref,
        b_in_ref,
        bias_ref,
        active_ref,
        grad_ref,
        small_ref,
        grad_qkv_out,
        grad_proj_out,
        grad_in_out,
        grad_out_out,
        w_qkv,
        w_proj,
        w_in,
        w_out,
        acc_qkv,
        acc_proj,
        acc_in,
        acc_out,
        mixed,
        attended,
        probs,
        hidden,
        slope,
        grad_att,
        grad_mixed,
        sems,
    ) = refs
    steps, patches, model = rows_ref.shape
    tiles = patches // tile
    held = (w_qkv, w_proj, w_in, w_out)
    totals = (acc_qkv, acc_proj, acc_in, acc_out)

    @pl.when(pl.program_id(0) == 0)
    def _():
        for idx in range(4):
            start_weight(groups[idx], table_ref, FROM_A, held[idx], sems.at[idx])
        for total in totals:
            total[...] = jnp.zeros_like(total)
        small_ref[...] = jnp.zeros_like(small_ref)
        for idx in range(4):
            wait_weight(held[idx], sems.at[idx])

    def gather_rows(ref):
        parts = [
            ref[:, idx * tile : (idx + 1) * tile, :].reshape(steps * tile, model)
            for idx in range(tiles)
        ]
        return jnp.concatenate(parts, 0)

    def spread_rows(ref, values):
        for idx in range(tiles):
            part = values[idx * steps * tile : (idx + 1) * steps * tile]
            ref[:, idx * tile : (idx + 1) * tile, :] = part.reshape(steps, tile, model).astype(
                ref.dtype
            )

    rows = gather_rows(rows_ref)
    unit_one, inverse_one = norm_stats(rows)
    normed_one = (unit_one * vec_ref[0:1] + vec_ref[1:2]).astype(BF)
    mixed[...] = dot(normed_one, w_qkv[...], 1, 0).astype(BF)
    span = steps * tile
    bias = bias_ref[...]
    for idx in range(tiles):
        tile_rows = slice(idx * span, (idx + 1) * span)

        def load(first):
            return mixed[tile_rows, first : first + LANES]

        def store(first, value):
            attended[tile_rows, first : first + LANES] = value

        def keep(head, value):
            probs[idx, head] = value

        attend_forward(load, model, store, keep, bias)
    middle = rows + dot(attended[...], w_proj[...], 1, 0)
    unit_two, inverse_two = norm_stats(middle)
    normed_two = (unit_two * vec_ref[2:3] + vec_ref[3:4]).astype(BF)
    result = middle + ff_through(normed_two, b_in_ref, w_in, w_out, hidden, slope)
    spread_rows(active_ref, result)

    from_own = pl.program_id(0) < pl.num_programs(0) // 2
    cotangent = jnp.where(from_own, own_ref[...], other_ref[...])
    grad_out = gather_rows(cotangent).astype(F32)
    grad_middle = ff_back(
        grad_out,
        normed_two,
        unit_two,
        inverse_two,
        vec_ref[2:3],
        w_in,
        w_out,
        hidden,
        slope,
        (acc_in, acc_out, small_ref),
    )
    proj_in = grad_middle.astype(BF)
    acc_proj[...] += dot(attended[...], proj_in, 0, 0)
    grad_att[...] = dot(proj_in, w_proj[...], 1, 1).astype(BF)
    for idx in range(tiles):
        tile_rows = slice(idx * span, (idx + 1) * span)

        def load(first):
            return mixed[tile_rows, first : first + LANES]

        def load_grad(first):
            return grad_att[tile_rows, first : first + LANES]

        def load_prob(head):
            return probs[idx, head]

        def store(first, value):
            grad_mixed[tile_rows, first : first + LANES] = value

        attend_backward(load, load_grad, load_prob, model, store)
    acc_qkv[...] += dot(normed_one, grad_mixed[...], 0, 0)
    grad_first = dot(grad_mixed[...], w_qkv[...], 1, 1)
    offset = 2 * model + w_in.shape[1]
    small_ref[:, offset : offset + model] += fold_rows(grad_first * unit_one)
    small_ref[:, offset + model : offset + 2 * model] += fold_rows(grad_first)
    spread_rows(
        grad_ref, grad_middle + norm_back(grad_first * vec_ref[0:1], unit_one, inverse_one)
    )

    @pl.when(pl.program_id(0) == pl.num_programs(0) - 1)
    def _():
        outs = (grad_qkv_out, grad_proj_out, grad_in_out, grad_out_out)
        places = (TO_B, TO_B, TO_A, TO_B)
        for idx in range(4):
            held[idx][...] = totals[idx][...].astype(BF)
            start_slabs(held[idx], table_ref, places[idx], outs[idx], sems.at[idx])
        for idx in range(4):
            wait_slabs(outs[idx], sems.at[idx])


ANY = pl.BlockSpec(memory_space=pl.ANY)
SMEM = pl.BlockSpec(memory_space=pltpu.SMEM)


def whole(shape):
    return pl.BlockSpec(shape, lambda idx: (0,) * len(shape))


def leading(shape):
    return pl.BlockSpec(shape, lambda idx: (idx,) + (0,) * (len(shape) - 1))


def limits(megabytes):
    return pltpu.CompilerParams(vmem_limit_bytes=megabytes * MIB)


def cost(flops, bytes_accessed):
    return pl.CostEstimate(flops=flops, bytes_accessed=bytes_accessed, transcendentals=0)


def spatial_forward(table, qkv_pieces, proj_pieces, own, other, vec):
    frames, half, model = own.shape
    patches = 2 * half
    each = min(2, frames)
    shape = jax.ShapeDtypeStruct
    return pl.pallas_call(
        functools.partial(spatial_forward_kernel, (len(qkv_pieces), len(proj_pieces))),
        grid=(frames // each,),
        in_specs=[SMEM]
        + [ANY] * (len(qkv_pieces) + len(proj_pieces))
        + [leading((each, half, model))] * 2
        + [whole(vec.shape)],
        out_specs=[
            leading((each, patches, model)),
            leading((each, patches, 3 * model)),
            leading((each, patches, model)),
            leading((each, HEADS, patches, patches)),
        ],
        out_shape=[
            shape((frames, patches, model), F32),
            shape((frames, patches, 3 * model), BF),
            shape((frames, patches, model), BF),
            shape((frames, HEADS, patches, patches), BF),
        ],
        scratch_shapes=[
            pltpu.VMEM((model, 3 * model), BF),
            pltpu.VMEM((model, model), BF),
            pltpu.SemaphoreType.DMA((2,)),
        ],
        compiler_params=limits(48),
        cost_estimate=cost(
            2 * frames * patches * model * (4 * model + 2 * patches), frames * patches * model * 24
        ),
        name="spatial_forward",
    )(table, *qkv_pieces, *proj_pieces, own, other, vec)


def feed_forward(table, in_pieces, out_pieces, middle, vec, b_in):
    tokens, model = middle.shape
    width = b_in.shape[1]
    block = min(512, tokens)
    shape = jax.ShapeDtypeStruct
    return pl.pallas_call(
        functools.partial(feed_forward_kernel, (len(in_pieces), len(out_pieces))),
        grid=(tokens // block,),
        in_specs=[SMEM]
        + [ANY] * (len(in_pieces) + len(out_pieces))
        + [leading((block, model)), whole(vec.shape), whole(b_in.shape)],
        out_specs=[leading((block, model)), leading((block, width)), leading((block, width))],
        out_shape=[
            shape((tokens, model), F32),
            shape((tokens, width), BF),
            shape((tokens, width), BF),
        ],
        scratch_shapes=[
            pltpu.VMEM((model, width), BF),
            pltpu.VMEM((width, model), BF),
            pltpu.SemaphoreType.DMA((2,)),
        ],
        compiler_params=limits(48),
        cost_estimate=cost(4 * tokens * model * width, tokens * (8 * model + 4 * width)),
        name="feed_forward",
    )(table, *in_pieces, *out_pieces, middle, vec, b_in)


def feed_backward(table, in_pieces, out_pieces, grad, middle, hidden, slope, vec, slabs):
    tokens, model = middle.shape
    width = hidden.shape[1]
    block = min(512, tokens)
    shape = jax.ShapeDtypeStruct
    small_width = 2 * model + width
    return pl.pallas_call(
        functools.partial(feed_backward_kernel, (len(in_pieces), len(out_pieces))),
        grid=(tokens // block,),
        in_specs=[SMEM]
        + [ANY] * (len(in_pieces) + len(out_pieces))
        + [leading((block, model))] * 2
        + [leading((block, width))] * 2
        + [whole(vec.shape)],
        out_specs=[leading((block, model)), whole((8, small_width)), ANY, ANY],
        out_shape=[
            shape((tokens, model), F32),
            shape((8, small_width), F32),
            shape((slabs, model // slabs, width), BF),
            shape((slabs, width // slabs, model), BF),
        ],
        scratch_shapes=[
            pltpu.VMEM((model, width), BF),
            pltpu.VMEM((width, model), BF),
            pltpu.VMEM((model, width), F32),
            pltpu.VMEM((width, model), F32),
            pltpu.SemaphoreType.DMA((2,)),
        ],
        compiler_params=limits(56),
        cost_estimate=cost(8 * tokens * model * width, tokens * (12 * model + 4 * width)),
        name="feed_backward",
    )(table, *in_pieces, *out_pieces, grad, middle, hidden, slope, vec)


def spatial_backward(table, qkv_pieces, proj_pieces, grad, own, other, mixed, attended, prob, vec, slabs):
    frames, half, model = own.shape
    patches = 2 * half
    each = min(2, frames)
    shape = jax.ShapeDtypeStruct
    return pl.pallas_call(
        functools.partial(spatial_backward_kernel, (len(qkv_pieces), len(proj_pieces))),
        grid=(frames // each,),
        in_specs=[SMEM]
        + [ANY] * (len(qkv_pieces) + len(proj_pieces))
        + [
            leading((each, patches, model)),
            leading((each, half, model)),
            leading((each, half, model)),
            leading((each, patches, 3 * model)),
            leading((each, patches, model)),
            leading((each, HEADS, patches, patches)),
            whole(vec.shape),
        ],
        out_specs=[
            leading((each, half, model)),
            leading((each, half, model)),
            whole((8, 2 * model)),
            ANY,
            ANY,
        ],
        out_shape=[
            shape((frames, half, model), BF),
            shape((frames, half, model), BF),
            shape((8, 2 * model), F32),
            shape((slabs, model // slabs, 3 * model), BF),
            shape((slabs, model // slabs, model), BF),
        ],
        scratch_shapes=[
            pltpu.VMEM((model, 3 * model), BF),
            pltpu.VMEM((model, model), BF),
            pltpu.VMEM((model, 3 * model), F32),
            pltpu.VMEM((model, model), F32),
            pltpu.VMEM((each * patches, model), BF),
            pltpu.VMEM((each * patches, 3 * model), BF),
            pltpu.SemaphoreType.DMA((2,)),
        ],
        compiler_params=limits(56),
        cost_estimate=cost(
            2 * frames * patches * model * (8 * model + 4 * patches), frames * patches * model * 30
        ),
        name="spatial_backward",
    )(table, *qkv_pieces, *proj_pieces, grad, own, other, mixed, attended, prob, vec)


def temporal_block(table, pieces, rows, own, other, vec, b_in, allowed, slabs):
    steps, patches, model = rows.shape
    width = b_in.shape[1]
    half = own.shape[1]
    each = min(64, half)
    tile = min(16, each)
    halves = half // each
    last = halves - 1
    count = steps * each
    same = jnp.eye(tile, dtype=jnp.bool_)
    bias = jnp.where(
        allowed.T[:, None, :, None] & same[None, :, None, :], 0.0, -1000000000.0
    ).astype(F32)
    bias = bias.reshape(steps * tile, steps * tile)
    shape = jax.ShapeDtypeStruct
    small_width = 4 * model + width
    block = (steps, each, model)
    return pl.pallas_call(
        functools.partial(temporal_kernel, tuple(len(piece) for piece in pieces), tile),
        grid=(2 * halves,),
        in_specs=[SMEM]
        + [ANY] * sum(len(piece) for piece in pieces)
        + [
            pl.BlockSpec(block, lambda idx: (0, idx, 0)),
            pl.BlockSpec(block, lambda idx: (0, jnp.minimum(idx, last), 0)),
            pl.BlockSpec(block, lambda idx: (0, jnp.maximum(idx - halves, 0), 0)),
            whole(vec.shape),
            whole(b_in.shape),
            whole(bias.shape),
        ],
        out_specs=[
            pl.BlockSpec(block, lambda idx: (0, idx, 0)),
            pl.BlockSpec(block, lambda idx: (0, idx, 0)),
            whole((8, small_width)),
            ANY,
            ANY,
            ANY,
            ANY,
        ],
        out_shape=[
            shape((steps, patches, model), BF),
            shape((steps, patches, model), F32),
            shape((8, small_width), F32),
            shape((slabs, model // slabs, 3 * model), BF),
            shape((slabs, model // slabs, model), BF),
            shape((slabs, model // slabs, width), BF),
            shape((slabs, width // slabs, model), BF),
        ],
        scratch_shapes=[
            pltpu.VMEM((model, 3 * model), BF),
            pltpu.VMEM((model, model), BF),
            pltpu.VMEM((model, width), BF),
            pltpu.VMEM((width, model), BF),
            pltpu.VMEM((model, 3 * model), F32),
            pltpu.VMEM((model, model), F32),
            pltpu.VMEM((model, width), F32),
            pltpu.VMEM((width, model), F32),
            pltpu.VMEM((count, 3 * model), BF),
            pltpu.VMEM((count, model), BF),
            pltpu.VMEM((each // tile, HEADS, steps * tile, steps * tile), BF),
            pltpu.VMEM((count, width), BF),
            pltpu.VMEM((count, width), BF),
            pltpu.VMEM((count, model), BF),
            pltpu.VMEM((count, 3 * model), BF),
            pltpu.SemaphoreType.DMA((4,)),
        ],
        compiler_params=limits(60),
        cost_estimate=cost(
            6 * steps * patches * model * (4 * model + 2 * width), steps * patches * model * 16
        ),
        name="temporal_block",
    )(
        table,
        *[item for piece in pieces for item in piece],
        rows,
        own,
        other,
        vec,
        b_in,
        bias,
    )


class Plan:
    def __init__(self, mesh):
        self.dp = mesh.shape["dp"]
        self.seq = mesh.shape["seq"]
        self.count = self.dp * self.seq
        self.cube = self.dp == 16 and self.seq == 2

    def swap(self, value, mask):
        pairs = [(idx, idx ^ mask) for idx in range(self.count)]
        return lax.ppermute(value, AXES, pairs)

    def me(self):
        return lax.axis_index("dp") * self.seq + lax.axis_index("seq")


ROW, CORE, COLUMN, Z_LOW, Z_HIGH = 1, 2, 4, 8, 16


def gather_masks(order):
    masks = [0]
    for stage in order:
        masks = masks + [mask ^ bit for bit in stage for mask in masks]
    return masks


STAGE_Z = (Z_LOW, Z_HIGH, Z_LOW | Z_HIGH)
GATHER_A = (STAGE_Z, (COLUMN,), (ROW,), (CORE,))
GATHER_B = (STAGE_Z, (ROW,), (COLUMN,), (CORE,))


def gather_pieces(plan, shards, order):
    if not plan.cube:
        return [
            [lax.all_gather(shard, AXES, axis=0, tiled=True)[None]] for shard in shards
        ]
    have = [shard[None] for shard in shards]
    for stage in order[:-1]:
        come = [[item] + [plan.swap(item, bit) for bit in stage] for item in have]
        have = [jnp.concatenate(parts, 0) for parts in come]
    return [[item, plan.swap(item, order[-1][0])] for item in have]


SUM_A = (CORE, COLUMN, ROW, Z_HIGH, Z_LOW)
SUM_B = (CORE, ROW, COLUMN, Z_HIGH, Z_LOW)


def sum_masks(order):
    masks = [0]
    for bit in reversed(order):
        masks = masks + [mask ^ bit for mask in masks]
    return masks


def add_up(*values):
    total = values[0].astype(F32)
    for value in values[1:]:
        total = total + value.astype(F32)
    return total


def scatter_sum(plan, slabs, order):
    if not plan.cube:
        return lax.psum_scatter(
            slabs[0].astype(F32), AXES, scatter_dimension=0, tiled=True
        )
    value = slabs
    for bit in order[:-2]:
        half = value.shape[0] // 2
        come = plan.swap(value[half:], bit)
        value = add_up(value[:half], come).astype(slabs.dtype)
    high, low = order[-2], order[-1]
    parts = [
        plan.swap(value[1], low),
        plan.swap(value[2], high),
        plan.swap(value[3], high ^ low),
    ]
    return add_up(value[0], *parts)


def to_frames(plan, values):
    steps, here, model = values.shape
    if plan.seq == 2:
        row = lax.axis_index("seq")
        count = steps // 2
        own = lax.dynamic_slice_in_dim(values, row * count, count, 0)
        away = lax.dynamic_slice_in_dim(values, (1 - row) * count, count, 0)
        return own, lax.ppermute(away, "seq", [(0, 1), (1, 0)])
    full = lax.all_to_all(values, "seq", split_axis=0, concat_axis=1, tiled=True)
    half = full.shape[1] // 2
    return full[:, :half], full[:, half:]


def from_frames(plan, own, other):
    if plan.seq == 2:
        row = lax.axis_index("seq")
        count = own.shape[0]
        come = lax.ppermute(other, "seq", [(0, 1), (1, 0)])
        first = jnp.where(row == 0, own, come)
        second = jnp.where(row == 0, come, own)
        return jnp.concatenate([first, second], 0)
    full = jnp.concatenate([own, other], 1)
    return lax.all_to_all(full, "seq", split_axis=1, concat_axis=0, tiled=True)


def regroup(plan, values, split_axis, concat_axis):
    members = plan.seq // MICRO
    if members == 1:
        return values
    row = lax.axis_index("seq")
    rank = row % members
    size = values.shape[split_axis] // members
    span = values.shape[concat_axis]
    shape = list(values.shape)
    shape[split_axis] = size
    shape[concat_axis] = span * members
    result = jnp.zeros(shape, values.dtype)
    for shift in range(members):
        target = (rank + shift) % members
        part = lax.dynamic_slice_in_dim(values, target * size, size, split_axis)
        if shift:
            pairs = [
                (idx, idx - idx % members + (idx + shift) % members) for idx in range(plan.seq)
            ]
            part = lax.ppermute(part, "seq", pairs)
        source = (rank - shift) % members
        result = lax.dynamic_update_slice_in_dim(result, part, source * span, concat_axis)
    return result


def clip_mask(lengths, steps):
    ends = jnp.cumsum(lengths, -1)
    positions = jnp.arange(steps, dtype=jnp.int32)
    clips = jnp.sum((positions[:, None] >= ends[None, :]).astype(jnp.int32), -1)
    return (clips[:, None] == clips[None, :]) & (positions[None, :] <= positions[:, None])


def on_device(plan, tokens, lengths, cotangent, norm_gain, norm_bias, w_qkv, w_proj, w_in, b_in, w_out):
    steps_all, here, model = tokens.shape[1:]
    steps = steps_all // MICRO
    width = b_in.shape[1] * plan.count
    row = lax.axis_index("seq")
    micro = row * MICRO // plan.seq
    allowed = clip_mask(lax.dynamic_index_in_dim(lengths[0], micro, 0, keepdims=False), steps)

    own, other = to_frames(plan, tokens[0])

    small = jnp.concatenate([norm_gain.reshape(-1), norm_bias.reshape(-1), b_in.reshape(-1)])
    if plan.cube:
        me = plan.me()
        orders = [gather_masks(GATHER_A), gather_masks(GATHER_B), sum_masks(SUM_A), sum_masks(SUM_B)]
        table = me ^ jnp.array(orders, jnp.int32)
        slabs = plan.count
        small = jnp.pad(small, (0, LANES * 16 - small.shape[0])).reshape(16, LANES)
        (small_pieces,) = gather_pieces(plan, [small], GATHER_A)
        small_all = jnp.concatenate(small_pieces, 0)[:, :2].reshape(plan.count, -1)
        pick = (table[FROM_A][None, :] == jnp.arange(plan.count)[:, None]).astype(BF)
        small_all = jnp.einsum("ij,jk->ik", pick, small_all, preferred_element_type=F32)
    else:
        table = jnp.zeros((4, 1), jnp.int32)
        slabs = 1
        small_all = lax.all_gather(small, AXES, axis=0).astype(F32)
    wide = model // plan.count
    cut = 4 * wide
    gains = small_all[:, :cut].reshape(plan.count, 2, 2, wide)
    shifts = small_all[:, cut : 2 * cut].reshape(plan.count, 2, 2, wide)
    gains = gains.transpose(1, 2, 0, 3).reshape(2, 2, model)
    shifts = shifts.transpose(1, 2, 0, 3).reshape(2, 2, model)
    vecs = jnp.stack([gains, shifts], 2).reshape(2, 4, model)
    biases = small_all[:, 2 * cut : 2 * cut + 2 * (width // plan.count)]
    biases = biases.reshape(plan.count, 2, -1).transpose(1, 0, 2).reshape(2, 1, width)

    qkv_0, proj_0 = gather_pieces(plan, [w_qkv[0], w_proj[0]], GATHER_A)
    (in_0,) = gather_pieces(plan, [w_in[0]], GATHER_A)
    (out_0,) = gather_pieces(plan, [w_out[0]], GATHER_B)
    qkv_1, proj_1, in_1, out_1 = gather_pieces(
        plan, [w_qkv[1], w_proj[1], w_in[1], w_out[1]], GATHER_A
    )

    middle, mixed, attended, prob = spatial_forward(table, qkv_0, proj_0, own, other, vecs[0])
    frames, patches = middle.shape[:2]
    count = frames * patches
    middle = middle.reshape(count, model)
    result, hidden, slope = feed_forward(table, in_0, out_0, middle, vecs[0], biases[0])

    ct_own, ct_other = to_frames(plan, cotangent[0])
    rows = regroup(plan, result.reshape(frames, patches, model), 1, 0)
    if plan.seq != 2:
        full = regroup(plan, jnp.concatenate([ct_own, ct_other], 1), 1, 0)
        cut_at = full.shape[1] // 2
        ct_own, ct_other = full[:, :cut_at], full[:, cut_at:]
    active, grad, small_1, g_qkv_1, g_proj_1, g_in_1, g_out_1 = temporal_block(
        table,
        (qkv_1, proj_1, in_1, out_1),
        rows,
        ct_own,
        ct_other,
        vecs[1],
        biases[1],
        allowed,
        slabs,
    )
    active = regroup(plan, active, 0, 1)
    half = active.shape[1] // 2
    activations = from_frames(plan, active[:, :half], active[:, half:])
    grad = regroup(plan, grad, 0, 1).reshape(count, model)

    s_in_1 = scatter_sum(plan, g_in_1, SUM_A)
    s_out_1 = scatter_sum(plan, g_out_1, SUM_B)
    s_qkv_1 = scatter_sum(plan, g_qkv_1, SUM_B)
    s_proj_1 = scatter_sum(plan, g_proj_1, SUM_B)

    grad_middle, small_0, g_in_0, g_out_0 = feed_backward(
        table, in_0, out_0, grad, middle, hidden, slope, vecs[0], slabs
    )
    s_in_0 = scatter_sum(plan, g_in_0, SUM_A)
    s_out_0 = scatter_sum(plan, g_out_0, SUM_B)
    grad_own, grad_other, tiny_0, g_qkv_0, g_proj_0 = spatial_backward(
        table,
        qkv_0,
        proj_0,
        grad_middle.reshape(frames, patches, model),
        own,
        other,
        mixed,
        attended,
        prob,
        vecs[0],
        slabs,
    )
    grad_tokens = from_frames(plan, grad_own, grad_other)
    s_qkv_0 = scatter_sum(plan, g_qkv_0, SUM_A)
    s_proj_0 = scatter_sum(plan, g_proj_0, SUM_A)

    small_0 = jnp.sum(small_0, 0)
    small_1 = jnp.sum(small_1, 0)
    tiny_0 = jnp.sum(tiny_0, 0)
    far = 2 * model + width

    def cut_up(values):
        return values.reshape(plan.count, -1)

    columns = [
        tiny_0[:model],
        small_0[:model],
        small_1[far : far + model],
        small_1[:model],
        tiny_0[model:],
        small_0[model : 2 * model],
        small_1[far + model :],
        small_1[model : 2 * model],
        small_0[2 * model :],
        small_1[2 * model : far],
    ]
    smalls = jnp.concatenate([cut_up(item) for item in columns], 1)
    if plan.cube:
        pick = (table[TO_A][:, None] == jnp.arange(plan.count)[None, :]).astype(F32)
        smalls = jnp.einsum(
            "ij,jk->ik", pick, smalls, preferred_element_type=F32, precision=lax.Precision.HIGHEST
        )
        mine = scatter_sum(plan, smalls.reshape(plan.count, 2, -1), SUM_A).reshape(-1)
    else:
        mine = lax.psum_scatter(smalls, AXES, scatter_dimension=0, tiled=True).reshape(-1)
    grad_gain = mine[:cut].reshape(2, 2, wide)
    grad_shift = mine[cut : 2 * cut].reshape(2, 2, wide)
    grad_b_in = mine[2 * cut :].reshape(2, -1)
    return (
        activations[None],
        grad_tokens[None],
        grad_gain,
        grad_shift,
        jnp.stack([s_qkv_0, s_qkv_1]),
        jnp.stack([s_proj_0, s_proj_1]),
        jnp.stack([s_in_0, s_in_1]),
        grad_b_in,
        jnp.stack([s_out_0, s_out_1]),
    )


def solution(mesh):
    in_specs = (
        P("dp", None, "seq", None),
        P("dp", None, None),
        P("dp", None, "seq", None),
        P(None, None, AXES),
        P(None, None, AXES),
        P(None, AXES, None),
        P(None, AXES, None),
        P(None, AXES, None),
        P(None, AXES),
        P(None, AXES, None),
    )
    out_specs = (
        P("dp", None, "seq", None),
        P("dp", None, "seq", None),
        P(None, None, AXES),
        P(None, None, AXES),
        P(None, AXES, None),
        P(None, AXES, None),
        P(None, AXES, None),
        P(None, AXES),
        P(None, AXES, None),
    )
    return jax.shard_map(
        functools.partial(on_device, Plan(mesh)),
        mesh=mesh,
        in_specs=in_specs,
        out_specs=out_specs,
        check_vma=False,
    )
```

time: 1900 us -> 587 us (0.31)
  waiting for transfers between devices: 864 us -> 135 us
  local copies, waits for them, and re-layouts: 357 us -> 60.4 us
  matrix products: 272 us -> 0.32 us
  Pallas kernels: 0 us -> 226 us
  blocking collectives: 211 us -> 0 us
  other arithmetic: 94.6 us -> 28.4 us
  starting transfers between devices: 69.3 us -> 128 us
    reduce_scatter x4 -> x0, waiting for transfers between devices: 623 us -> none  [the longest x1 186 us: on_device(): lax.psum_scatter(merged[4], ('dp', 'seq'), scatter_dimension=1, tiled=True)]
    dot_general x64 -> x2, matrix products: 272 us -> 0.32 us  [the longest x1 0.2 us: on_device(): jnp.einsum('ij,jk->ik', pick, smalls, preferred_element_type=F32, precisi...]
    pallas_call x0 -> x5, Pallas kernels: none -> 226 us  [the longest x1 116 us: temporal_block(): pl.pallas_call(functools.partial(temporal_kernel, tuple((len(piece) for p...]
    unnamed x14 -> x0, waiting for transfers between devices: 219 us -> none
    all_gather x3 -> x0, blocking collectives: 211 us -> none  [the longest x1 74.1 us: on_device(): lax.all_gather(b_in, ('dp', 'seq'), axis=1, tiled=True)]
    ppermute x0 -> x112, waiting for transfers between devices: none -> 135 us  [the longest x108 96.4 us: swap(): return lax.ppermute(value, AXES, pairs)]
    ppermute x0 -> x112, starting transfers between devices: none -> 128 us  [the longest x108 124 us: swap(): return lax.ppermute(value, AXES, pairs)]
    unnamed x409 -> x167, local copies, waits for them, and re-layouts: 119 us -> 26.1 us
  transfers between devices with their start and end apart: 27 -> 112, of which waited for: 11 -> 38; matrix products, arithmetic and copies ran while one was open for 21% -> 14% of each run, Pallas kernels for 0% -> 7%
where the time goes in v1:
time: 587 us; the launch traced here: 580 us
  Pallas kernels  226 us (39%)
  waiting for transfers between devices  135 us (23%)
  starting transfers between devices  128 us (22%)
  local copies, waits for them, and re-layouts  60.4 us (10%)
  other arithmetic  28.4 us (5%)
    ppermute x108, starting transfers between devices, swap(): return lax.ppermute(value, AXES, pairs)  124 us
    pallas_call x1, Pallas kernels, temporal_block(): pl.pallas_call(functools.partial(temporal_kernel, tuple((len(piece) for p...  116 us
    ppermute x108, waiting for transfers between devices, swap(): return lax.ppermute(value, AXES, pairs)  96.4 us
    ppermute x2, waiting for transfers between devices, from_frames(): come = lax.ppermute(other, 'seq', [(0, 1), (1, 0)])  38.6 us
    pallas_call x1, Pallas kernels, spatial_backward(): pl.pallas_call(functools.partial(spatial_backward_kernel, (len(qkv_pieces...  37.4 us
    pallas_call x1, Pallas kernels, feed_backward(): pl.pallas_call(functools.partial(feed_backward_kernel, (len(in_pieces), l...  29.5 us
    unnamed x167, local copies, waits for them, and re-layouts  26.1 us
    pallas_call x1, Pallas kernels, feed_forward(): pl.pallas_call(functools.partial(feed_forward_kernel, (len(in_pieces), le...  23.6 us
  transfers between devices with their start and end apart: 112, of which 38 were waited for; matrix products, arithmetic and copies ran while one was open for 14% of the time, Pallas kernels for 7%

profile of v1, /device:TPU:0, one launch (start us, length us, event | category | flops | bytes accessed | tf_op | source)
XLA Modules:
  0.0 580.0 jit_solution(9772684850044463209)
XLA Ops:
  3.0 5.0 collective-permute-start.51
  10.1 3.7 collective-permute-start.44
  16.7 2.8 dynamic-slice_bitcast_fusion.2
  19.6 1.5 dynamic-slice_bitcast_fusion
  24.9 1.9 select_n.51.refs_13_
  27.5 3.7 collective-permute-start.8
  35.7 3.7 collective-permute-start.38
  44.1 3.7 collective-permute-start.2
  53.5 3.7 collective-permute-start.26
  61.4 3.7 collective-permute-start.14
  65.1 1.5 collective-permute-start.53
  71.5 3.6 collective-permute-start.32
  78.6 3.6 collective-permute-start.20
  102.9 4.0 collective-permute-done.46
  109.9 1.6 constant_dynamic-update-slice_fusion.16.refs_2_
  112.7 1.7 constant_dynamic-update-slice_fusion
  115.1 1.7 constant_dynamic-update-slice_fusion.66
  116.9 3.2 collective-permute-done.27
  121.2 2.7 collective-permute-done.33
  127.7 4.6 collective-permute-done.40
  135.2 8.3 %collective-permute-done.28 = bf16[8,16,2048]{2,1,0:T(8,128)(2,1)S(1)} collective-permute-done((bf16[8,16,2048]{2,1,0:T(8,128)(2,1)}, bf16[8,16,2048]{2,1,0:T(8,128)(2,1)S(1)}, u32[]{:S(2)}, u32[]{:S(2)}) %collective-permute-start.28) | collective-permute-done | bytes 524320 | tf_op jit(solution)/shard_map/ppermute | solution.py:791
  143.6 8.4 %collective-permute-done.4 = bf16[8,16,1536]{2,1,0:T(8,128)(2,1)S(1)} collective-permute-done((bf16[8,16,1536]{2,1,0:T(8,128)(2,1)S(1)}, bf16[8,16,1536]{2,1,0:T(8,128)(2,1)S(1)}, u32[]{:S(2)}, u32[]{:S(2)}) %collective-permute-start.4) | collective-permute-done | bytes 393248 | tf_op jit(solution)/shard_map/ppermute | solution.py:791
  151.9 11.2 %collective-permute-done.16 = bf16[8,16,2048]{2,1,0:T(8,128)(2,1)S(1)} collective-permute-done((bf16[8,16,2048]{2,1,0:T(8,128)(2,1)S(1)}, bf16[8,16,2048]{2,1,0:T(8,128)(2,1)S(1)}, u32[]{:S(2)}, u32[]{:S(2)}) %collective-permute-start.16) | collective-permute-done | bytes 524320 | tf_op jit(solution)/shard_map/ppermute | solution.py:791
  163.2 6.2 %collective-permute-done.22 = bf16[8,64,512]{2,1,0:T(8,128)(2,1)S(1)} collective-permute-done((bf16[8,64,512]{2,1,0:T(8,128)(2,1)S(1)}, bf16[8,64,512]{2,1,0:T(8,128)(2,1)S(1)}, u32[]{:S(2)}, u32[]{:S(2)}) %collective-permute-start.22) | collective-permute-done | bytes 524320 | tf_op jit(solution)/shard_map/ppermute | solution.py:791
  172.2 19.1 %spatial_forward.1 = (f32[8,256,512]{2,1,0:T(8,128)}, bf16[8,256,1536]{2,1,0:T(8,128)(2,1)}, bf16[8,256,512]{2,1,0:T(8,128)(2,1)}, bf16[8,8,256,256]{3,2,1,0:T(8,128)(2,1)}) custom-call(s32[4,32]{1,0:T(4,128)S(1)} %broadcast_xor_fusion.table_ref, bf16[16,16,1536]{2,1,0:T(8,128)(2,1)S(1)} %constant_dynamic-update-slice_fusion.71.refs_0_, ...), custom_call_target="tpu_custom_call" | custom-call | flops 5368709120 | bytes 25165824 | tf_op jit(solution)/shard_map/spatial_forward/pallas_call | solution.py:555
  192.1 23.6 %feed_forward.1 = (f32[2048,512]{1,0:T(8,128)}, bf16[2048,2048]{1,0:T(8,128)(2,1)}, bf16[2048,2048]{1,0:T(8,128)(2,1)}) custom-call(s32[4,32]{1,0:T(4,128)S(1)} %broadcast_xor_fusion.table_ref, bf16[16,16,2048]{2,1,0:T(8,128)(2,1)S(1)} %constant_dynamic-update-slice_fusion.49.refs_0_, bf16[16,16,2048]{2,1,0:T(8,128)(2,1)S(1)} %collective-permute-done.29.refs_1_, ...), custom_call_target="tpu_custom_call" | custom-call | flops 8589934592 | bytes 25165824 | tf_op jit(solution)/shard_map/feed_forward/pallas_call | solution.py:592
  217.4 115.9 %temporal_block.1 = (bf16[8,256,512]{2,1,0:T(8,128)(2,1)}, f32[8,256,512]{2,1,0:T(8,128)}, f32[8,4096]{1,0:T(8,128)}, bf16[32,16,1536]{2,1,0:T(8,128)(2,1)}, bf1...) custom-call(s32[4,32]{1,0:T(4,128)} %copy-done.4, ...), custom_call_target="tpu_custom_call" | custom-call | flops 38654705664 | bytes 16777216 | tf_op jit(solution)/shard_map/temporal_block/pallas_call | solution.py:716
  333.3 29.5 %feed_backward.1 = (f32[2048,512]{1,0:T(8,128)}, f32[8,3072]{1,0:T(8,128)}, bf16[32,16,2048]{2,1,0:T(8,128)(2,1)}, bf16[32,64,512]{2,1,0:T(8,128)(2,1)}) custom-call(s32[4,32]{1,0:T(4,128)} %copy-done.4, bf16[16,16,2048]{2,1,0:T(8,128)(2,1)} %copy-done.6, bf16[16,16,2048]{2,1,0:T(8,128)(2,1)} %copy-done.10, bf16[16,64,512]{2,1,0:T(8,128)(2,1)} %copy-done.5, ...), custom_call_target="tpu_custom_call" | custom-call | flops 17179869184 | bytes 29360128 | tf_op jit(solution)/shard_map/feed_backward/pallas_call | solution.py:621
  363.9 37.4 %spatial_backward.1 = (bf16[8,128,512]{2,1,0:T(8,128)(2,1)}, bf16[8,128,512]{2,1,0:T(8,128)(2,1)}, f32[8,1024]{1,0:T(8,128)}, bf16[32,16,1536]{2,1,0:T(8,128)(2,1)}, bf16[32,16,512]{2,1,0:T(8,128)(2,1)}) custom-call(s32[4,32]{1,0:T(4,128)} %copy-done.4, bf16[16,16,1536]{2,1,0:T(8,128)(2,1)} %copy-done.8, bf16[16,16,1536]{2,1,0:T(8,128)(2,1)} %copy-done.12, ...), custom_call_target="tpu_custom_call" | custom-call | flops 10737418240 | bytes 31457280 | tf_op jit(solution)/shard_map/spatial_backward/pallas_call | solution.py:654
  404.7 1.6 collective-permute-start.59
  406.3 2.2 collective-permute-done.59
  409.8 1.8 slice.545
  413.4 2.7 collective-permute-start.63
  417.8 2.2 slice.535
  431.0 1.6 collective-permute-start.77
  434.0 1.6 collective-permute-start.84
  438.4 1.5 collective-permute-start.85
  439.9 2.7 collective-permute-start.87
  445.4 2.7 collective-permute-start.81
  448.3 2.7 collective-permute-done.81
  451.0 1.8 collective-permute-done.80
  456.5 1.7 add_convert_fusion.5
  461.4 17.6 %collective-permute-done.56 = bf16[8,128,512]{2,1,0:T(8,128)(2,1)S(1)} collective-permute-done((bf16[8,128,512]{2,1,0:T(8,128)(2,1)S(1)}, bf16[8,128,512]{2,1,0:T(8,128)(2,1)S(1)}, u32[]{:S(2)}, u32[]{:S(2)}) %collective-permute-start.56) | collective-permute-done | bytes 1048608 | tf_op jit(solution)/shard_map/ppermute | solution.py:878
  480.4 21.0 %collective-permute-done.57 = bf16[8,128,512]{2,1,0:T(8,128)(2,1)S(1)} collective-permute-done((bf16[8,128,512]{2,1,0:T(8,128)(2,1)S(1)}, bf16[8,128,512]{2,1,0:T(8,128)(2,1)S(1)}, u32[]{:S(2)}, u32[]{:S(2)}) %collective-permute-start.57) | collective-permute-done | bytes 1048608 | tf_op jit(solution)/shard_map/ppermute | solution.py:878
  502.6 1.6 collective-permute-start.95
  508.0 1.8 collective-permute-done.71
  512.7 3.7 collective-permute-done.72
  516.6 3.6 collective-permute-start.75
  520.2 2.7 collective-permute-done.66
  523.3 3.1 collective-permute-start.67
  528.9 1.6 collective-permute-start.101
  530.5 1.8 collective-permute-done.69
  538.0 5.3 collective-permute-done.101
  544.5 2.6 collective-permute-done.89
  548.4 3.9 collective-permute-done.108
  554.6 2.9 collective-permute-start.99
  557.8 1.8 collective-permute-done.97
  561.2 3.7 collective-permute-start.103
  564.9 1.9 collective-permute-done.98
  566.8 2.5 collective-permute-start.105
  569.4 1.9 collective-permute-start.91
  571.3 2.5 collective-permute-start.93
  575.3 2.0 collective-permute-done.93
  577.3 1.7 collective-permute-done.92
  (503 shorter events, 138.1 us)
Async XLA Ops:
  3.0 23.8 %collective-permute-start.51 = (bf16[1,16,128]{2,1,0:T(8,128)(2,1)S(1)}, bf16[1,16,128]{2,1,0:T(8,128)(2,1)S(1)}, u32[]{:S(2)}, u32[]{:S(2)}) collective-permute-start(bf16[1,16,128]{2,1,0:T(8,128)(2,1)S(1)} %fusion.35), channel_id=1, source_target_pairs={{0,24},{1,25},{2,26},{3,27},{4,28},{5,29},{6,30},{7,31},{8,16},{9,... | collective-permute-start | bytes 12296 | tf_op jit(solution)/shard_map/ppermute | solution.py:791
  8.1 19.4 %collective-permute-start.50 = (bf16[1,16,128]{2,1,0:T(8,128)(2,1)S(1)}, bf16[1,16,128]{2,1,0:T(8,128)(2,1)S(1)}, u32[]{:S(2)}, u32[]{:S(2)}) collective-permute-start(bf16[1,16,128]{2,1,0:T(8,128)(2,1)S(1)} %fusion.35), channel_id=1, source_target_pairs={{0,16},{1,17},{2,18},{3,19},{4,20},{5,21},{6,22},{7,23},{8,24},{9,... | collective-permute-start | bytes 12296 | tf_op jit(solution)/shard_map/ppermute | solution.py:791
  8.1 23.1 %collective-permute-start.49 = (bf16[1,16,128]{2,1,0:T(8,128)(2,1)S(1)}, bf16[1,16,128]{2,1,0:T(8,128)(2,1)}, u32[]{:S(2)}, u32[]{:S(2)}) collective-permute-start(bf16[1,16,128]{2,1,0:T(8,128)(2,1)S(1)} %fusion.35), channel_id=1, source_target_pairs={{0,8},{1,9},{2,10},{3,11},{4,12},{5,13},{6,14},{7,15},{8,0},{9,1},... | collective-permute-start | bytes 12296 | tf_op jit(solution)/shard_map/ppermute | solution.py:791
  10.1 25.6 %collective-permute-start.44 = (bf16[1,16,512]{2,1,0:T(8,128)(2,1)}, bf16[1,16,512]{2,1,0:T(8,128)(2,1)}, u32[]{:S(2)}, u32[]{:S(2)}) collective-permute-start(bf16[1,16,512]{2,1,0:T(8,128)(2,1)} %get-tuple-element.169), channel_id=1, source_target_pairs={{0,24},{1,25},{2,26},{3,27},{4,28},{5,29},{6,30},{7,31},{8,16},{9,... | collective-permute-start | bytes 49160 | tf_op jit(solution)/shard_map/ppermute | solution.py:791
  13.9 25.6 %collective-permute-start.43 = (bf16[1,16,512]{2,1,0:T(8,128)(2,1)}, bf16[1,16,512]{2,1,0:T(8,128)(2,1)}, u32[]{:S(2)}, u32[]{:S(2)}) collective-permute-start(bf16[1,16,512]{2,1,0:T(8,128)(2,1)} %get-tuple-element.169), channel_id=1, source_target_pairs={{0,16},{1,17},{2,18},{3,19},{4,20},{5,21},{6,22},{7,23},{8,24},{9,... | collective-permute-start | bytes 49160 | tf_op jit(solution)/shard_map/ppermute | solution.py:791
  27.5 16.6 %collective-permute-start.8 = (bf16[1,16,512]{2,1,0:T(8,128)(2,1)}, bf16[1,16,512]{2,1,0:T(8,128)(2,1)S(1)}, u32[]{:S(2)}, u32[]{:S(2)}) collective-permute-start(bf16[1,16,512]{2,1,0:T(8,128)(2,1)} %get-tuple-element.170), channel_id=1, source_target_pairs={{0,24},{1,25},{2,26},{3,27},{4,28},{5,29},{6,30},{7,31},{8,16},{9,... | collective-permute-start | bytes 49160 | tf_op jit(solution)/shard_map/ppermute | solution.py:791
  31.2 16.6 %collective-permute-start.7 = (bf16[1,16,512]{2,1,0:T(8,128)(2,1)}, bf16[1,16,512]{2,1,0:T(8,128)(2,1)S(1)}, u32[]{:S(2)}, u32[]{:S(2)}) collective-permute-start(bf16[1,16,512]{2,1,0:T(8,128)(2,1)} %get-tuple-element.170), channel_id=1, source_target_pairs={{0,16},{1,17},{2,18},{3,19},{4,20},{5,21},{6,22},{7,23},{8,24},{9,... | collective-permute-start | bytes 49160 | tf_op jit(solution)/shard_map/ppermute | solution.py:791
  35.7 17.8 %collective-permute-start.38 = (bf16[1,16,1536]{2,1,0:T(8,128)(2,1)}, bf16[1,16,1536]{2,1,0:T(8,128)(2,1)S(1)}, u32[]{:S(2)}, u32[]{:S(2)}) collective-permute-start(bf16[1,16,1536]{2,1,0:T(8,128)(2,1)} %get-tuple-element.109), channel_id=1, source_target_pairs={{0,24},{1,25},{2,26},{3,27},{4,28},{5,29},{6,30},{7,31},{8,16},{9,... | collective-permute-start | bytes 147464 | tf_op jit(solution)/shard_map/ppermute | solution.py:791
  39.4 17.8 %collective-permute-start.37 = (bf16[1,16,1536]{2,1,0:T(8,128)(2,1)}, bf16[1,16,1536]{2,1,0:T(8,128)(2,1)S(1)}, u32[]{:S(2)}, u32[]{:S(2)}) collective-permute-start(bf16[1,16,1536]{2,1,0:T(8,128)(2,1)} %get-tuple-element.109), channel_id=1, source_target_pairs={{0,16},{1,17},{2,18},{3,19},{4,20},{5,21},{6,22},{7,23},{8,24},{9,... | collective-permute-start | bytes 147464 | tf_op jit(solution)/shard_map/ppermute | solution.py:791
  44.1 17.3 %collective-permute-start.2 = (bf16[1,16,1536]{2,1,0:T(8,128)(2,1)}, bf16[1,16,1536]{2,1,0:T(8,128)(2,1)S(1)}, u32[]{:S(2)}, u32[]{:S(2)}) collective-permute-start(bf16[1,16,1536]{2,1,0:T(8,128)(2,1)} %get-tuple-element.110), channel_id=1, source_target_pairs={{0,24},{1,25},{2,26},{3,27},{4,28},{5,29},{6,30},{7,31},{8,16},{9,... | collective-permute-start | bytes 147464 | tf_op jit(solution)/shard_map/ppermute | solution.py:791
  51.6 13.5 %collective-permute-start.1 = (bf16[1,16,1536]{2,1,0:T(8,128)(2,1)}, bf16[1,16,1536]{2,1,0:T(8,128)(2,1)S(1)}, u32[]{:S(2)}, u32[]{:S(2)}) collective-permute-start(bf16[1,16,1536]{2,1,0:T(8,128)(2,1)} %get-tuple-element.110), channel_id=1, source_target_pairs={{0,16},{1,17},{2,18},{3,19},{4,20},{5,21},{6,22},{7,23},{8,24},{9,... | collective-permute-start | bytes 147464 | tf_op jit(solution)/shard_map/ppermute | solution.py:791
  53.5 18.0 %collective-permute-start.26 = (bf16[1,16,2048]{2,1,0:T(8,128)(2,1)}, bf16[1,16,2048]{2,1,0:T(8,128)(2,1)S(1)}, u32[]{:S(2)}, u32[]{:S(2)}) collective-permute-start(bf16[1,16,2048]{2,1,0:T(8,128)(2,1)} %get-tuple-element.103), channel_id=1, source_target_pairs={{0,24},{1,25},{2,26},{3,27},{4,28},{5,29},{6,30},{7,31},{8,16},{9,... | collective-permute-start | bytes 196616 | tf_op jit(solution)/shard_map/ppermute | solution.py:791
  57.3 17.9 %collective-permute-start.25 = (bf16[1,16,2048]{2,1,0:T(8,128)(2,1)}, bf16[1,16,2048]{2,1,0:T(8,128)(2,1)S(1)}, u32[]{:S(2)}, u32[]{:S(2)}) collective-permute-start(bf16[1,16,2048]{2,1,0:T(8,128)(2,1)} %get-tuple-element.103), channel_id=1, source_target_pairs={{0,16},{1,17},{2,18},{3,19},{4,20},{5,21},{6,22},{7,23},{8,24},{9,... | collective-permute-start | bytes 196616 | tf_op jit(solution)/shard_map/ppermute | solution.py:791
  61.4 17.2 %collective-permute-start.14 = (bf16[1,16,2048]{2,1,0:T(8,128)(2,1)}, bf16[1,16,2048]{2,1,0:T(8,128)(2,1)S(1)}, u32[]{:S(2)}, u32[]{:S(2)}) collective-permute-start(bf16[1,16,2048]{2,1,0:T(8,128)(2,1)} %get-tuple-element.104), channel_id=1, source_target_pairs={{0,24},{1,25},{2,26},{3,27},{4,28},{5,29},{6,30},{7,31},{8,16},{9,... | collective-permute-start | bytes 196616 | tf_op jit(solution)/shard_map/ppermute | solution.py:791
  69.4 12.8 %collective-permute-start.13 = (bf16[1,16,2048]{2,1,0:T(8,128)(2,1)S(1)}, bf16[1,16,2048]{2,1,0:T(8,128)(2,1)S(1)}, u32[]{:S(2)}, u32[]{:S(2)}) collective-permute-start(bf16[1,16,2048]{2,1,0:T(8,128)(2,1)S(1)} %copy-done.33), channel_id=1, source_target_pairs={{0,16},{1,17},{2,18},{3,19},{4,20},{5,21},{6,22},{7,23},{8,24},{9,... | collective-permute-start | bytes 196616 | tf_op jit(solution)/shard_map/ppermute | solution.py:791
  71.5 14.2 %collective-permute-start.32 = (bf16[1,64,512]{2,1,0:T(8,128)(2,1)S(1)}, bf16[1,64,512]{2,1,0:T(8,128)(2,1)S(1)}, u32[]{:S(2)}, u32[]{:S(2)}) collective-permute-start(bf16[1,64,512]{2,1,0:T(8,128)(2,1)S(1)} %get-tuple-element.97), channel_id=1, source_target_pairs={{0,24},{1,25},{2,26},{3,27},{4,28},{5,29},{6,30},{7,31},{8,16},{9,... | collective-permute-start | bytes 196616 | tf_op jit(solution)/shard_map/ppermute | solution.py:791
  75.1 11.9 %collective-permute-start.31 = (bf16[1,64,512]{2,1,0:T(8,128)(2,1)S(1)}, bf16[1,64,512]{2,1,0:T(8,128)(2,1)S(1)}, u32[]{:S(2)}, u32[]{:S(2)}) collective-permute-start(bf16[1,64,512]{2,1,0:T(8,128)(2,1)S(1)} %get-tuple-element.97), channel_id=1, source_target_pairs={{0,16},{1,17},{2,18},{3,19},{4,20},{5,21},{6,22},{7,23},{8,24},{9,... | collective-permute-start | bytes 196616 | tf_op jit(solution)/shard_map/ppermute | solution.py:791
  78.6 13.1 %collective-permute-start.20 = (bf16[1,64,512]{2,1,0:T(8,128)(2,1)S(1)}, bf16[1,64,512]{2,1,0:T(8,128)(2,1)S(1)}, u32[]{:S(2)}, u32[]{:S(2)}) collective-permute-start(bf16[1,64,512]{2,1,0:T(8,128)(2,1)S(1)} %get-tuple-element.98), channel_id=1, source_target_pairs={{0,24},{1,25},{2,26},{3,27},{4,28},{5,29},{6,30},{7,31},{8,16},{9,... | collective-permute-start | bytes 196616 | tf_op jit(solution)/shard_map/ppermute | solution.py:791
  82.2 11.0 %collective-permute-start.19 = (bf16[1,64,512]{2,1,0:T(8,128)(2,1)S(1)}, bf16[1,64,512]{2,1,0:T(8,128)(2,1)S(1)}, u32[]{:S(2)}, u32[]{:S(2)}) collective-permute-start(bf16[1,64,512]{2,1,0:T(8,128)(2,1)S(1)} %get-tuple-element.98), channel_id=1, source_target_pairs={{0,16},{1,17},{2,18},{3,19},{4,20},{5,21},{6,22},{7,23},{8,24},{9,... | collective-permute-start | bytes 196616 | tf_op jit(solution)/shard_map/ppermute | solution.py:791
  85.7 86.0 %collective-permute-start.48 = (bf16[8,128,512]{2,1,0:T(8,128)(2,1)}, bf16[8,128,512]{2,1,0:T(8,128)(2,1)}, u32[]{:S(2)}, u32[]{:S(2)}) collective-permute-start(bf16[8,128,512]{2,1,0:T(8,128)(2,1)} %get-tuple-element.61), channel_id=1, source_target_pairs={{0,1},{1,0},{2,3},{3,2},{4,5},{5,4},{6,7},{7,6},{8,9},{9,8},{10,11... | collective-permute-start | bytes 3145736 | tf_op jit(solution)/shard_map/ppermute | solution.py:868
  91.7 19.7 %collective-permute-start.3 = (bf16[4,16,1536]{2,1,0:T(8,128)(2,1)}, bf16[4,16,1536]{2,1,0:T(8,128)(2,1)}, u32[]{:S(2)}, u32[]{:S(2)}) collective-permute-start(bf16[4,16,1536]{2,1,0:T(8,128)(2,1)} %pad_maximum_fusion.6), channel_id=1, source_target_pairs={{0,4},{1,5},{2,6},{3,7},{4,0},{5,1},{6,2},{7,3},{8,12},{9,13},{10,... | collective-permute-start | bytes 589832 | tf_op jit(solution)/shard_map/ppermute | solution.py:791
  93.2 21.2 %collective-permute-start.39 = (bf16[4,16,1536]{2,1,0:T(8,128)(2,1)}, bf16[4,16,1536]{2,1,0:T(8,128)(2,1)}, u32[]{:S(2)}, u32[]{:S(2)}) collective-permute-start(bf16[4,16,1536]{2,1,0:T(8,128)(2,1)} %pad_maximum_fusion.7), channel_id=1, source_target_pairs={{0,4},{1,5},{2,6},{3,7},{4,0},{5,1},{6,2},{7,3},{8,12},{9,13},{10,... | collective-permute-start | bytes 589832 | tf_op jit(solution)/shard_map/ppermute | solution.py:791
  96.5 10.4 %collective-permute-start.46 = (bf16[8,16,512]{2,1,0:T(8,128)(2,1)}, bf16[8,16,512]{2,1,0:T(8,128)(2,1)}, u32[]{:S(2)}, u32[]{:S(2)}) collective-permute-start(bf16[8,16,512]{2,1,0:T(8,128)(2,1)} %get-tuple-element.117), channel_id=1, source_target_pairs={{0,1},{1,0},{2,3},{3,2},{4,5},{5,4},{6,7},{7,6},{8,9},{9,8},{10,11... | collective-permute-start | bytes 393224 | tf_op jit(solution)/shard_map/ppermute | solution.py:791
  97.8 11.1 %collective-permute-start.10 = (bf16[8,16,512]{2,1,0:T(8,128)(2,1)}, bf16[8,16,512]{2,1,0:T(8,128)(2,1)}, u32[]{:S(2)}, u32[]{:S(2)}) collective-permute-start(bf16[8,16,512]{2,1,0:T(8,128)(2,1)} %get-tuple-element.143), channel_id=1, source_target_pairs={{0,1},{1,0},{2,3},{3,2},{4,5},{5,4},{6,7},{7,6},{8,9},{9,8},{10,11... | collective-permute-start | bytes 393224 | tf_op jit(solution)/shard_map/ppermute | solution.py:791
  106.9 17.8 %collective-permute-start.15 = (bf16[4,16,2048]{2,1,0:T(8,128)(2,1)}, bf16[4,16,2048]{2,1,0:T(8,128)(2,1)S(1)}, u32[]{:S(2)}, u32[]{:S(2)}) collective-permute-start(bf16[4,16,2048]{2,1,0:T(8,128)(2,1)} %pad_maximum_fusion), channel_id=1, source_target_pairs={{0,4},{1,5},{2,6},{3,7},{4,0},{5,1},{6,2},{7,3},{8,12},{9,13},{10,... | collective-permute-start | bytes 786440 | tf_op jit(solution)/shard_map/ppermute | solution.py:791
  109.0 11.1 %collective-permute-start.27 = (bf16[4,16,2048]{2,1,0:T(8,128)(2,1)}, bf16[4,16,2048]{2,1,0:T(8,128)(2,1)S(1)}, u32[]{:S(2)}, u32[]{:S(2)}) collective-permute-start(bf16[4,16,2048]{2,1,0:T(8,128)(2,1)} %pad_maximum_fusion.2), channel_id=1, source_target_pairs={{0,4},{1,5},{2,6},{3,7},{4,0},{5,1},{6,2},{7,3},{8,12},{9,13},{10,... | collective-permute-start | bytes 786440 | tf_op jit(solution)/shard_map/ppermute | solution.py:791
  111.5 14.9 %collective-permute-start.21 = (bf16[4,64,512]{2,1,0:T(8,128)(2,1)}, bf16[4,64,512]{2,1,0:T(8,128)(2,1)S(1)}, u32[]{:S(2)}, u32[]{:S(2)}) collective-permute-start(bf16[4,64,512]{2,1,0:T(8,128)(2,1)} %pad_maximum_fusion.1), channel_id=1, source_target_pairs={{0,4},{1,5},{2,6},{3,7},{4,0},{5,1},{6,2},{7,3},{8,12},{9,13},{10,... | collective-permute-start | bytes 786440 | tf_op jit(solution)/shard_map/ppermute | solution.py:791
  120.1 12.2 %collective-permute-start.40 = (bf16[8,16,1536]{2,1,0:T(8,128)(2,1)}, bf16[8,16,1536]{2,1,0:T(8,128)(2,1)S(1)}, u32[]{:S(2)}, u32[]{:S(2)}) collective-permute-start(bf16[8,16,1536]{2,1,0:T(8,128)(2,1)} %get-tuple-element.89), channel_id=1, source_target_pairs={{0,1},{1,0},{2,3},{3,2},{4,5},{5,4},{6,7},{7,6},{8,9},{9,8},{10,11... | collective-permute-start | bytes 1179656 | tf_op jit(solution)/shard_map/ppermute | solution.py:791
  123.8 19.7 %collective-permute-start.28 = (bf16[8,16,2048]{2,1,0:T(8,128)(2,1)}, bf16[8,16,2048]{2,1,0:T(8,128)(2,1)S(1)}, u32[]{:S(2)}, u32[]{:S(2)}) collective-permute-start(bf16[8,16,2048]{2,1,0:T(8,128)(2,1)} %get-tuple-element.77), channel_id=1, source_target_pairs={{0,1},{1,0},{2,3},{3,2},{4,5},{5,4},{6,7},{7,6},{8,9},{9,8},{10,11... | collective-permute-start | bytes 1572872 | tf_op jit(solution)/shard_map/ppermute | solution.py:791
  126.3 25.6 %collective-permute-start.4 = (bf16[8,16,1536]{2,1,0:T(8,128)(2,1)S(1)}, bf16[8,16,1536]{2,1,0:T(8,128)(2,1)S(1)}, u32[]{:S(2)}, u32[]{:S(2)}) collective-permute-start(bf16[8,16,1536]{2,1,0:T(8,128)(2,1)S(1)} %copy-done.43), channel_id=1, source_target_pairs={{0,1},{1,0},{2,3},{3,2},{4,5},{5,4},{6,7},{7,6},{8,9},{9,8},{10,11... | collective-permute-start | bytes 1179656 | tf_op jit(solution)/shard_map/ppermute | solution.py:791
  132.3 30.9 %collective-permute-start.16 = (bf16[8,16,2048]{2,1,0:T(8,128)(2,1)S(1)}, bf16[8,16,2048]{2,1,0:T(8,128)(2,1)S(1)}, u32[]{:S(2)}, u32[]{:S(2)}) collective-permute-start(bf16[8,16,2048]{2,1,0:T(8,128)(2,1)S(1)} %get-tuple-element.81), channel_id=1, source_target_pairs={{0,1},{1,0},{2,3},{3,2},{4,5},{5,4},{6,7},{7,6},{8,9},{9,8},{10,11... | collective-permute-start | bytes 1572872 | tf_op jit(solution)/shard_map/ppermute | solution.py:791
  133.9 35.5 %collective-permute-start.22 = (bf16[8,64,512]{2,1,0:T(8,128)(2,1)S(1)}, bf16[8,64,512]{2,1,0:T(8,128)(2,1)S(1)}, u32[]{:S(2)}, u32[]{:S(2)}) collective-permute-start(bf16[8,64,512]{2,1,0:T(8,128)(2,1)S(1)} %get-tuple-element.79), channel_id=1, source_target_pairs={{0,1},{1,0},{2,3},{3,2},{4,5},{5,4},{6,7},{7,6},{8,9},{9,8},{10,11... | collective-permute-start | bytes 1572872 | tf_op jit(solution)/shard_map/ppermute | solution.py:791
  143.5 28.2 %collective-permute-start.41 = (bf16[16,16,1536]{2,1,0:T(8,128)(2,1)S(1)}, bf16[16,16,1536]{2,1,0:T(8,128)(2,1)S(1)}, u32[]{:S(2)}, u32[]{:S(2)}) collective-permute-start(bf16[16,16,1536]{2,1,0:T(8,128)(2,1)S(1)} %constant_dynamic-update-slice_fusion.71.refs_0_), channel_id=1, source_target_pairs={{0,2},{1,3},{2,0},{3,1},{4,6},{5,7},{6,4},{7,5},{8,10},{9,11},{10,... | collective-permute-start | bytes 2359304 | tf_op jit(solution)/shard_map/ppermute | solution.py:791
  151.9 39.4 %collective-permute-start.29 = (bf16[16,16,2048]{2,1,0:T(8,128)(2,1)S(1)}, bf16[16,16,2048]{2,1,0:T(8,128)(2,1)S(1)}, u32[]{:S(2)}, u32[]{:S(2)}) collective-permute-start(bf16[16,16,2048]{2,1,0:T(8,128)(2,1)S(1)} %constant_dynamic-update-slice_fusion.49.refs_0_), channel_id=1, source_target_pairs={{0,2},{1,3},{2,0},{3,1},{4,6},{5,7},{6,4},{7,5},{8,10},{9,11},{10,... | collective-permute-start | bytes 3145736 | tf_op jit(solution)/shard_map/ppermute | solution.py:791
  163.2 28.5 %collective-permute-start.35 = (bf16[16,64,512]{2,1,0:T(8,128)(2,1)S(1)}, bf16[16,64,512]{2,1,0:T(8,128)(2,1)S(1)}, u32[]{:S(2)}, u32[]{:S(2)}) collective-permute-start(bf16[16,64,512]{2,1,0:T(8,128)(2,1)S(1)} %constant_dynamic-update-slice_fusion.60.refs_2_), channel_id=1, source_target_pairs={{0,2},{1,3},{2,0},{3,1},{4,6},{5,7},{6,4},{7,5},{8,10},{9,11},{10,... | collective-permute-start | bytes 3145736 | tf_op jit(solution)/shard_map/ppermute | solution.py:791
  171.0 44.8 %collective-permute-start.55 = (bf16[8,128,512]{2,1,0:T(8,128)(2,1)S(1)}, bf16[8,128,512]{2,1,0:T(8,128)(2,1)S(1)}, u32[]{:S(2)}, u32[]{:S(2)}) collective-permute-start(bf16[8,128,512]{2,1,0:T(8,128)(2,1)S(1)} %copy-done.27), channel_id=1, source_target_pairs={{0,1},{1,0},{2,3},{3,2},{4,5},{5,4},{6,7},{7,6},{8,9},{9,8},{10,11... | collective-permute-start | bytes 3145736 | tf_op jit(solution)/shard_map/ppermute | solution.py:868
  171.7 44.1 %collective-permute-start.17 = (bf16[16,16,2048]{2,1,0:T(8,128)(2,1)S(1)}, bf16[16,16,2048]{2,1,0:T(8,128)(2,1)S(1)}, u32[]{:S(2)}, u32[]{:S(2)}) collective-permute-start(bf16[16,16,2048]{2,1,0:T(8,128)(2,1)S(1)} %constant_dynamic-update-slice_fusion.27.refs_4_), channel_id=1, source_target_pairs={{0,2},{1,3},{2,0},{3,1},{4,6},{5,7},{6,4},{7,5},{8,10},{9,11},{10,... | collective-permute-start | bytes 3145736 | tf_op jit(solution)/shard_map/ppermute | solution.py:791
  171.7 44.1 %collective-permute-start.23 = (bf16[16,64,512]{2,1,0:T(8,128)(2,1)S(1)}, bf16[16,64,512]{2,1,0:T(8,128)(2,1)}, u32[]{:S(2)}, u32[]{:S(2)}) collective-permute-start(bf16[16,64,512]{2,1,0:T(8,128)(2,1)S(1)} %constant_dynamic-update-slice_fusion.38.refs_6_), channel_id=1, source_target_pairs={{0,2},{1,3},{2,0},{3,1},{4,6},{5,7},{6,4},{7,5},{8,10},{9,11},{10,... | collective-permute-start | bytes 3145736 | tf_op jit(solution)/shard_map/ppermute | solution.py:791
  191.4 24.3 %collective-permute-start.11 = (bf16[16,16,512]{2,1,0:T(8,128)(2,1)S(1)}, bf16[16,16,512]{2,1,0:T(8,128)(2,1)S(1)}, u32[]{:S(2)}, u32[]{:S(2)}) collective-permute-start(bf16[16,16,512]{2,1,0:T(8,128)(2,1)S(1)} %copy-done.60), channel_id=1, source_target_pairs={{0,2},{1,3},{2,0},{3,1},{4,6},{5,7},{6,4},{7,5},{8,10},{9,11},{10,... | collective-permute-start | bytes 786440 | tf_op jit(solution)/shard_map/ppermute | solution.py:791
  191.6 24.1 %collective-permute-start.5 = (bf16[16,16,1536]{2,1,0:T(8,128)(2,1)S(1)}, bf16[16,16,1536]{2,1,0:T(8,128)(2,1)S(1)}, u32[]{:S(2)}, u32[]{:S(2)}) collective-permute-start(bf16[16,16,1536]{2,1,0:T(8,128)(2,1)S(1)} %constant_dynamic-update-slice_fusion.5.refs_0_), channel_id=1, source_target_pairs={{0,2},{1,3},{2,0},{3,1},{4,6},{5,7},{6,4},{7,5},{8,10},{9,11},{10,... | collective-permute-start | bytes 2359304 | tf_op jit(solution)/shard_map/ppermute | solution.py:791
  412.1 13.1 %collective-permute-start.61 = (f32[2,128]{1,0:T(2,128)S(1)}, f32[2,128]{1,0:T(2,128)S(1)}, u32[]{:S(2)}, u32[]{:S(2)}) collective-permute-start(f32[2,128]{1,0:T(2,128)S(1)} %get-tuple-element.196), channel_id=1, source_target_pairs={{0,8},{1,9},{2,10},{3,11},{4,12},{5,13},{6,14},{7,15},{8,0},{9,1},... | collective-permute-start | bytes 3080 | tf_op jit(solution)/shard_map/ppermute | solution.py:791
  413.4 11.9 %collective-permute-start.63 = (f32[2,128]{1,0:T(2,128)S(1)}, f32[2,128]{1,0:T(2,128)S(1)}, u32[]{:S(2)}, u32[]{:S(2)}) collective-permute-start(f32[2,128]{1,0:T(2,128)S(1)} %get-tuple-element.197), channel_id=1, source_target_pairs={{0,24},{1,25},{2,26},{3,27},{4,28},{5,29},{6,30},{7,31},{8,16},{9,... | collective-permute-start | bytes 3080 | tf_op jit(solution)/shard_map/ppermute | solution.py:791
  416.3 10.8 %collective-permute-start.82 = (bf16[16,16,512]{2,1,0:T(8,128)(2,1)S(1)}, bf16[16,16,512]{2,1,0:T(8,128)(2,1)}, u32[]{:S(2)}, u32[]{:S(2)}) collective-permute-start(bf16[16,16,512]{2,1,0:T(8,128)(2,1)S(1)} %slice.555), channel_id=1, source_target_pairs={{0,2},{1,3},{2,0},{3,1},{4,6},{5,7},{6,4},{7,5},{8,10},{9,11},{10,... | collective-permute-start | bytes 786440 | tf_op jit(solution)/shard_map/ppermute | solution.py:791
  416.3 13.5 %collective-permute-start.76 = (bf16[16,16,512]{2,1,0:T(8,128)(2,1)}, bf16[16,16,512]{2,1,0:T(8,128)(2,1)}, u32[]{:S(2)}, u32[]{:S(2)}) collective-permute-start(bf16[16,16,512]{2,1,0:T(8,128)(2,1)} %slice.545), channel_id=1, source_target_pairs={{0,2},{1,3},{2,0},{3,1},{4,6},{5,7},{6,4},{7,5},{8,10},{9,11},{10,... | collective-permute-start | bytes 786440 | tf_op jit(solution)/shard_map/ppermute | solution.py:791
  425.2 29.3 %collective-permute-start.70 = (bf16[16,16,1536]{2,1,0:T(8,128)(2,1)}, bf16[16,16,1536]{2,1,0:T(8,128)(2,1)}, u32[]{:S(2)}, u32[]{:S(2)}) collective-permute-start(bf16[16,16,1536]{2,1,0:T(8,128)(2,1)} %slice.535), channel_id=1, source_target_pairs={{0,2},{1,3},{2,0},{3,1},{4,6},{5,7},{6,4},{7,5},{8,10},{9,11},{10,... | collective-permute-start | bytes 2359304 | tf_op jit(solution)/shard_map/ppermute | solution.py:791
  425.3 30.7 %collective-permute-start.64 = (bf16[16,16,1536]{2,1,0:T(8,128)(2,1)}, bf16[16,16,1536]{2,1,0:T(8,128)(2,1)}, u32[]{:S(2)}, u32[]{:S(2)}) collective-permute-start(bf16[16,16,1536]{2,1,0:T(8,128)(2,1)} %slice.525), channel_id=1, source_target_pairs={{0,2},{1,3},{2,0},{3,1},{4,6},{5,7},{6,4},{7,5},{8,10},{9,11},{10,... | collective-permute-start | bytes 2359304 | tf_op jit(solution)/shard_map/ppermute | solution.py:791
  452.8 26.1 %collective-permute-start.56 = (bf16[8,128,512]{2,1,0:T(8,128)(2,1)S(1)}, bf16[8,128,512]{2,1,0:T(8,128)(2,1)S(1)}, u32[]{:S(2)}, u32[]{:S(2)}) collective-permute-start(bf16[8,128,512]{2,1,0:T(8,128)(2,1)S(1)} %copy-done.30), channel_id=1, source_target_pairs={{0,1},{1,0},{2,3},{3,2},{4,5},{5,4},{6,7},{7,6},{8,9},{9,8},{10,11... | collective-permute-start | bytes 3145736 | tf_op jit(solution)/shard_map/ppermute | solution.py:878
  454.5 50.0 %collective-permute-start.100 = (bf16[16,64,512]{2,1,0:T(8,128)(2,1)S(1)}, bf16[16,64,512]{2,1,0:T(8,128)(2,1)S(1)}, u32[]{:S(2)}, u32[]{:S(2)}) collective-permute-start(bf16[16,64,512]{2,1,0:T(8,128)(2,1)S(1)} %slice.586), channel_id=1, source_target_pairs={{0,2},{1,3},{2,0},{3,1},{4,6},{5,7},{6,4},{7,5},{8,10},{9,11},{10,... | collective-permute-start | bytes 3145736 | tf_op jit(solution)/shard_map/ppermute | solution.py:791
  456.0 46.6 %collective-permute-start.88 = (bf16[16,16,2048]{2,1,0:T(8,128)(2,1)S(1)}, bf16[16,16,2048]{2,1,0:T(8,128)(2,1)S(1)}, u32[]{:S(2)}, u32[]{:S(2)}) collective-permute-start(bf16[16,16,2048]{2,1,0:T(8,128)(2,1)S(1)} %copy-done.29), channel_id=1, source_target_pairs={{0,2},{1,3},{2,0},{3,1},{4,6},{5,7},{6,4},{7,5},{8,10},{9,11},{10,... | collective-permute-start | bytes 3145736 | tf_op jit(solution)/shard_map/ppermute | solution.py:791
  458.3 43.1 %collective-permute-start.57 = (bf16[8,128,512]{2,1,0:T(8,128)(2,1)S(1)}, bf16[8,128,512]{2,1,0:T(8,128)(2,1)S(1)}, u32[]{:S(2)}, u32[]{:S(2)}) collective-permute-start(bf16[8,128,512]{2,1,0:T(8,128)(2,1)S(1)} %copy-done.62), channel_id=1, source_target_pairs={{0,1},{1,0},{2,3},{3,2},{4,5},{5,4},{6,7},{7,6},{8,9},{9,8},{10,11... | collective-permute-start | bytes 3145736 | tf_op jit(solution)/shard_map/ppermute | solution.py:878
  459.8 50.0 %collective-permute-start.71 = (bf16[8,16,1536]{2,1,0:T(8,128)(2,1)S(1)}, bf16[8,16,1536]{2,1,0:T(8,128)(2,1)S(1)}, u32[]{:S(2)}, u32[]{:S(2)}) collective-permute-start(bf16[8,16,1536]{2,1,0:T(8,128)(2,1)S(1)} %slice.642), channel_id=1, source_target_pairs={{0,1},{1,0},{2,3},{3,2},{4,5},{5,4},{6,7},{7,6},{8,9},{9,8},{10,11... | collective-permute-start | bytes 1179656 | tf_op jit(solution)/shard_map/ppermute | solution.py:791
  478.9 32.3 %collective-permute-start.65 = (bf16[8,16,1536]{2,1,0:T(8,128)(2,1)S(1)}, bf16[8,16,1536]{2,1,0:T(8,128)(2,1)S(1)}, u32[]{:S(2)}, u32[]{:S(2)}) collective-permute-start(bf16[8,16,1536]{2,1,0:T(8,128)(2,1)S(1)} %slice.634), channel_id=1, source_target_pairs={{0,4},{1,5},{2,6},{3,7},{4,0},{5,1},{6,2},{7,3},{8,12},{9,13},{10,... | collective-permute-start | bytes 1179656 | tf_op jit(solution)/shard_map/ppermute | solution.py:791
  501.4 33.6 %collective-permute-start.107 = (bf16[8,64,512]{2,1,0:T(8,128)(2,1)S(1)}, bf16[8,64,512]{2,1,0:T(8,128)(2,1)S(1)}, u32[]{:S(2)}, u32[]{:S(2)}) collective-permute-start(bf16[8,64,512]{2,1,0:T(8,128)(2,1)S(1)} %slice.690), channel_id=1, source_target_pairs={{0,1},{1,0},{2,3},{3,2},{4,5},{5,4},{6,7},{7,6},{8,9},{9,8},{10,11... | collective-permute-start | bytes 1572872 | tf_op jit(solution)/shard_map/ppermute | solution.py:791
  502.6 33.9 %collective-permute-start.95 = (bf16[8,16,2048]{2,1,0:T(8,128)(2,1)S(1)}, bf16[8,16,2048]{2,1,0:T(8,128)(2,1)S(1)}, u32[]{:S(2)}, u32[]{:S(2)}) collective-permute-start(bf16[8,16,2048]{2,1,0:T(8,128)(2,1)S(1)} %slice.674), channel_id=1, source_target_pairs={{0,4},{1,5},{2,6},{3,7},{4,0},{5,1},{6,2},{7,3},{8,12},{9,13},{10,... | collective-permute-start | bytes 1572872 | tf_op jit(solution)/shard_map/ppermute | solution.py:791
  511.3 11.6 %collective-permute-start.66 = (bf16[4,16,1536]{2,1,0:T(8,128)(2,1)S(1)}, bf16[4,16,1536]{2,1,0:T(8,128)(2,1)S(1)}, u32[]{:S(2)}, u32[]{:S(2)}) collective-permute-start(bf16[4,16,1536]{2,1,0:T(8,128)(2,1)S(1)} %slice.636), channel_id=1, source_target_pairs={{0,1},{1,0},{2,3},{3,2},{4,5},{5,4},{6,7},{7,6},{8,9},{9,8},{10,11... | collective-permute-start | bytes 589832 | tf_op jit(solution)/shard_map/ppermute | solution.py:791
  528.9 14.4 %collective-permute-start.101 = (bf16[8,64,512]{2,1,0:T(8,128)(2,1)S(1)}, bf16[8,64,512]{2,1,0:T(8,128)(2,1)S(1)}, u32[]{:S(2)}, u32[]{:S(2)}) collective-permute-start(bf16[8,64,512]{2,1,0:T(8,128)(2,1)S(1)} %slice.682), channel_id=1, source_target_pairs={{0,1},{1,0},{2,3},{3,2},{4,5},{5,4},{6,7},{7,6},{8,9},{9,8},{10,11... | collective-permute-start | bytes 1572872 | tf_op jit(solution)/shard_map/ppermute | solution.py:791
  532.3 14.9 %collective-permute-start.89 = (bf16[8,16,2048]{2,1,0:T(8,128)(2,1)S(1)}, bf16[8,16,2048]{2,1,0:T(8,128)(2,1)S(1)}, u32[]{:S(2)}, u32[]{:S(2)}) collective-permute-start(bf16[8,16,2048]{2,1,0:T(8,128)(2,1)S(1)} %slice.666), channel_id=1, source_target_pairs={{0,4},{1,5},{2,6},{3,7},{4,0},{5,1},{6,2},{7,3},{8,12},{9,13},{10,... | collective-permute-start | bytes 1572872 | tf_op jit(solution)/shard_map/ppermute | solution.py:791
  535.2 17.1 %collective-permute-start.108 = (bf16[4,64,512]{2,1,0:T(8,128)(2,1)S(1)}, bf16[4,64,512]{2,1,0:T(8,128)(2,1)S(1)}, u32[]{:S(2)}, u32[]{:S(2)}) collective-permute-start(bf16[4,64,512]{2,1,0:T(8,128)(2,1)S(1)} %slice.692), channel_id=1, source_target_pairs={{0,4},{1,5},{2,6},{3,7},{4,0},{5,1},{6,2},{7,3},{8,12},{9,13},{10,... | collective-permute-start | bytes 786440 | tf_op jit(solution)/shard_map/ppermute | solution.py:791
  536.6 16.7 %collective-permute-start.96 = (bf16[4,16,2048]{2,1,0:T(8,128)(2,1)S(1)}, bf16[4,16,2048]{2,1,0:T(8,128)(2,1)S(1)}, u32[]{:S(2)}, u32[]{:S(2)}) collective-permute-start(bf16[4,16,2048]{2,1,0:T(8,128)(2,1)S(1)} %slice.676), channel_id=1, source_target_pairs={{0,1},{1,0},{2,3},{3,2},{4,5},{5,4},{6,7},{7,6},{8,9},{9,8},{10,11... | collective-permute-start | bytes 786440 | tf_op jit(solution)/shard_map/ppermute | solution.py:791
  543.4 14.2 %collective-permute-start.102 = (bf16[4,64,512]{2,1,0:T(8,128)(2,1)S(1)}, bf16[4,64,512]{2,1,0:T(8,128)(2,1)S(1)}, u32[]{:S(2)}, u32[]{:S(2)}) collective-permute-start(bf16[4,64,512]{2,1,0:T(8,128)(2,1)S(1)} %slice.684), channel_id=1, source_target_pairs={{0,4},{1,5},{2,6},{3,7},{4,0},{5,1},{6,2},{7,3},{8,12},{9,13},{10,... | collective-permute-start | bytes 786440 | tf_op jit(solution)/shard_map/ppermute | solution.py:791
  552.3 17.0 %collective-permute-start.109 = (bf16[64,512]{1,0:T(8,128)(2,1)S(1)}, bf16[64,512]{1,0:T(8,128)(2,1)S(1)}, u32[]{:S(2)}, u32[]{:S(2)}) collective-permute-start(bf16[64,512]{1,0:T(8,128)(2,1)S(1)} %get-tuple-element.66), channel_id=1, source_target_pairs={{0,8},{1,9},{2,10},{3,11},{4,12},{5,13},{6,14},{7,15},{8,0},{9,1},... | collective-permute-start | bytes 196616 | tf_op jit(solution)/shard_map/ppermute | solution.py:791
  552.7 16.7 %collective-permute-start.111 = (bf16[64,512]{1,0:T(8,128)(2,1)S(1)}, bf16[64,512]{1,0:T(8,128)(2,1)S(1)}, u32[]{:S(2)}, u32[]{:S(2)}) collective-permute-start(bf16[64,512]{1,0:T(8,128)(2,1)S(1)} %get-tuple-element.67), channel_id=1, source_target_pairs={{0,24},{1,25},{2,26},{3,27},{4,28},{5,29},{6,30},{7,31},{8,16},{9,... | collective-permute-start | bytes 196616 | tf_op jit(solution)/shard_map/ppermute | solution.py:791
  559.6 11.6 %collective-permute-start.110 = (bf16[64,512]{1,0:T(8,128)(2,1)S(1)}, bf16[64,512]{1,0:T(8,128)(2,1)S(1)}, u32[]{:S(2)}, u32[]{:S(2)}) collective-permute-start(bf16[64,512]{1,0:T(8,128)(2,1)S(1)} %get-tuple-element.68), channel_id=1, source_target_pairs={{0,16},{1,17},{2,18},{3,19},{4,20},{5,21},{6,22},{7,23},{8,24},{9,... | collective-permute-start | bytes 196616 | tf_op jit(solution)/shard_map/ppermute | solution.py:791
  561.2 12.6 %collective-permute-start.103 = (bf16[64,512]{1,0:T(8,128)(2,1)S(1)}, bf16[64,512]{1,0:T(8,128)(2,1)S(1)}, u32[]{:S(2)}, u32[]{:S(2)}) collective-permute-start(bf16[64,512]{1,0:T(8,128)(2,1)S(1)} %get-tuple-element.63), channel_id=1, source_target_pairs={{0,8},{1,9},{2,10},{3,11},{4,12},{5,13},{6,14},{7,15},{8,0},{9,1},... | collective-permute-start | bytes 196616 | tf_op jit(solution)/shard_map/ppermute | solution.py:791
  (115 other events, 1944.2 us)
